TPU v7x, 512 devices: a whole 4x4x16 slice. The times are simulated.
512 devices in a mesh: leaf: 64 (over z, y), sec: 8 (over x, core).
Axes of the slice: x: 4, y: 4, z: 16, core: 2. Of those that a mesh axis runs over, the one named last changes fastest.
Arguments:
- leaf_inv: bfloat16 [524288, 1024], P(('leaf', 'sec')), may hold values from -0.1875 to 0.1875
- subtree_blocks: int32 [64, 8], P('leaf', 'sec'), may hold values from 1 to 8
- subtree_shift_rhs: bfloat16 [524288, 128], P(('leaf', 'sec')), may hold values from -6 to 6
- leaf_noise: bfloat16 [524288, 128], P(('leaf', 'sec')), may hold values from -6 to 6
- leaf_dev: bfloat16 [524288], P(('leaf', 'sec')), may hold values from 0.29882812 to 3
- sep_inv: bfloat16 [16384, 3584], P(('leaf', 'sec')), may hold values from -0.1875 to 0.1875
- sep_panel: bfloat16 [16384, 3584], P(('leaf', 'sec')), may hold values from -0.1875 to 0.1875
- sep_rhs: bfloat16 [3, 16384, 128], P(None, ('leaf', 'sec')), may hold values from -6 to 6
- sep_noise: bfloat16 [3, 16384, 128], P(None, ('leaf', 'sec')), may hold values from -6 to 6
- sep_dev: bfloat16 [3, 16384], P(None, ('leaf', 'sec')), may hold values from 0.29882812 to 3
Outputs:
- subtree_scaled_samples: bfloat16 [524288, 128], P(('leaf', 'sec'))
- sep_sample: bfloat16 [3, 16384, 128], P(None, ('leaf', 'sec'))
All inputs are finite; a program needn't handle non-finite values.
Results may differ from a plain program's by a relative error of at most 0.019.
Values may be sent and summed in bfloat16 or wider, within the bound.
A program may use at most 64 MiB of HBM per device.

v0:
```python
import jax
import jax.numpy as jnp
from jax import lax
from jax.sharding import PartitionSpec as P

BLOCK = 128


def from_partner(block, axis, apart):
    count = lax.axis_size(axis)
    route = []
    for low in range(count):
        high = low | 1 << apart
        if high != low and high < count:
            route += [(low, high), (high, low)]
    return lax.ppermute(block, axis, route)


def pair_gather(block, height):
    leaf_place = lax.axis_index("leaf")
    for bit_index in range(height):
        partner = from_partner(block, "leaf", bit_index)
        upper_half = leaf_place >> bit_index & 1 == 1
        block = jnp.where(
            upper_half, jnp.concatenate([partner, block], 0), jnp.concatenate([block, partner], 0)
        )
    return block


def group_gather(piece, height):
    block = lax.all_gather(piece, "sec", axis=0, tiled=True)
    return pair_gather(block, height)


def halve_pairs(partial_sum, height):
    leaf_place = lax.axis_index("leaf")
    for bit_index in reversed(range(height)):
        half_rows = partial_sum.shape[0] // 2
        lower_rows = partial_sum[:half_rows]
        upper_rows = partial_sum[half_rows:]
        upper_half = leaf_place >> bit_index & 1 == 1
        kept = jnp.where(upper_half, upper_rows, lower_rows)
        outgoing = jnp.where(upper_half, lower_rows, upper_rows)
        partial_sum = kept + from_partner(outgoing, "leaf", bit_index)
    return partial_sum


def group_reduce(partial_sum, height):
    reduced = halve_pairs(partial_sum, height)
    return lax.psum_scatter(reduced, "sec", scatter_dimension=0, tiled=True)


def transposed_product(matrix, vector):
    return lax.dot_general(
        matrix, vector, (((0,), (0,)), ((), ())), preferred_element_type=jnp.float32
    )


def on_device(
    leaf_inv,
    subtree_blocks,
    subtree_shift_rhs,
    leaf_noise,
    leaf_dev,
    sep_inv,
    sep_panel,
    sep_rhs,
    sep_noise,
    sep_dev,
):
    subtree_row_count = leaf_inv.shape[0]
    row_count = sep_inv.shape[0]
    levels = sep_rhs.shape[0]
    sections = lax.axis_size("sec")
    active_rows = subtree_blocks[0, 0] * BLOCK
    row_positions = jnp.arange(subtree_row_count, dtype=jnp.int32)
    row_activity = (row_positions >= subtree_row_count - active_rows)[:, None]
    subtree_shifted = jnp.where(
        row_activity, subtree_shift_rhs, jnp.zeros((), subtree_shift_rhs.dtype)
    )
    forward_subtree = jnp.dot(leaf_inv, subtree_shifted, preferred_element_type=jnp.float32)
    subtree_forward_solution = jnp.where(row_activity, forward_subtree, jnp.float32(0.0)).astype(
        jnp.bfloat16
    )
    top = subtree_forward_solution[subtree_row_count - row_count :]
    solved = []
    for height in range(1, levels + 1):
        span = 2**height * sections * row_count
        offset = (2**height - 2) * sections * row_count
        children = group_gather(top, height)
        panel = sep_panel[:, offset : offset + span]
        inverse_block = sep_inv[:, offset : offset + span]
        reduced = (
            sep_rhs[height - 1].astype(jnp.float32)
            - jnp.dot(panel, children, preferred_element_type=jnp.float32)
        ).astype(jnp.bfloat16)
        whole_reduced = group_gather(reduced, height)
        result = jnp.dot(inverse_block, whole_reduced, preferred_element_type=jnp.float32).astype(
            jnp.bfloat16
        )
        solved.append(result)
        top = result
    samples = [None] * levels
    correction = None
    for height in range(levels, 0, -1):
        span = 2**height * sections * row_count
        offset = (2**height - 2) * sections * row_count
        panel = sep_panel[:, offset : offset + span]
        inverse_block = sep_inv[:, offset : offset + span]
        summed = solved[height - 1].astype(jnp.float32) + sep_noise[height - 1].astype(jnp.float32)
        if correction is not None:
            summed = summed - correction
        vector = summed.astype(jnp.bfloat16)
        backed = group_reduce(transposed_product(inverse_block, vector), height).astype(
            jnp.bfloat16
        )
        samples[height - 1] = (
            sep_dev[height - 1][:, None].astype(jnp.float32) * backed.astype(jnp.float32)
        ).astype(jnp.bfloat16)
        correction = group_reduce(transposed_product(panel, backed), height)
    leading = jnp.zeros((subtree_row_count - row_count, correction.shape[1]), jnp.float32)
    placed = jnp.concatenate([leading, correction], axis=0)
    subtree_summed = (
        subtree_forward_solution.astype(jnp.float32) + leaf_noise.astype(jnp.float32) - placed
    )
    subtree_weight = jnp.where(row_activity, subtree_summed, jnp.float32(0.0)).astype(jnp.bfloat16)
    subtree_solution = transposed_product(leaf_inv, subtree_weight)
    sample_scales = leaf_dev[:, None].astype(jnp.float32)
    subtree_scaled_samples = jnp.where(
        row_activity, sample_scales * subtree_solution, jnp.float32(0.0)
    ).astype(jnp.bfloat16)
    return (subtree_scaled_samples, jnp.stack(samples))


def solution(mesh):
    in_specs = (
        P(("leaf", "sec"), None),
        P("leaf", "sec"),
        P(("leaf", "sec"), None),
        P(("leaf", "sec"), None),
        P(("leaf", "sec")),
        P(("leaf", "sec"), None),
        P(("leaf", "sec"), None),
        P(None, ("leaf", "sec"), None),
        P(None, ("leaf", "sec"), None),
        P(None, ("leaf", "sec")),
    )
    out_specs = (P(("leaf", "sec"), None), P(None, ("leaf", "sec"), None))
    return jax.shard_map(
        on_device, mesh=mesh, in_specs=in_specs, out_specs=out_specs, check_vma=False
    )
```

profile of v0, /device:TPU:1, one launch (start us, length us, event | category | flops | bytes accessed | tf_op | source)
XLA Modules:
  0.0 543.1 jit_solution(11738488947053809435)
XLA Ops:
  10.1 19.4 %all_gather.18 = bf16[256,128]{1,0:T(8,128)(2,1)S(1)} all-gather(bf16[32,128]{1,0:T(8,128)(2,1)S(1)} %copy.28), channel_id=1, replica_groups=mesh['leaf'=64,'sec'=8] {'sec'}, dimensions={0}, use_global_device_ids=true | all-gather | bytes 73728 | tf_op jit(solution)/shard_map/all_gather | solution.py:31
  35.1 13.5 %all_gather.19 = bf16[256,128]{1,0:T(8,128)(2,1)S(1)} all-gather(bf16[32,128]{1,0:T(8,128)(2,1)S(1)} %fusion.8), channel_id=1, replica_groups=mesh['leaf'=64,'sec'=8] {'sec'}, dimensions={0}, use_global_device_ids=true | all-gather | bytes 73728 | tf_op jit(solution)/shard_map/all_gather | solution.py:31
  55.0 13.5 %all_gather.20 = bf16[256,128]{1,0:T(8,128)(2,1)S(1)} all-gather(bf16[32,128]{1,0:T(8,128)(2,1)S(1)} %fusion.15), channel_id=1, replica_groups=mesh['leaf'=64,'sec'=8] {'sec'}, dimensions={0}, use_global_device_ids=true | all-gather | bytes 73728 | tf_op jit(solution)/shard_map/all_gather | solution.py:31
  75.9 5.3 collective-permute-done.3
  81.4 14.7 %all_gather.21 = bf16[256,128]{1,0:T(8,128)(2,1)S(1)} all-gather(bf16[32,128]{1,0:T(8,128)(2,1)S(1)} %fusion.9), channel_id=1, replica_groups=mesh['leaf'=64,'sec'=8] {'sec'}, dimensions={0}, use_global_device_ids=true | all-gather | bytes 73728 | tf_op jit(solution)/shard_map/all_gather | solution.py:31
  103.4 5.3 collective-permute-done.5
  109.8 14.7 %all_gather.22 = bf16[256,128]{1,0:T(8,128)(2,1)S(1)} all-gather(bf16[32,128]{1,0:T(8,128)(2,1)S(1)} %fusion.16), channel_id=1, replica_groups=mesh['leaf'=64,'sec'=8] {'sec'}, dimensions={0}, use_global_device_ids=true | all-gather | bytes 73728 | tf_op jit(solution)/shard_map/all_gather | solution.py:31
  131.8 5.3 collective-permute-done.7
  139.1 5.6 %collective-permute-done.8 = bf16[1024,128]{1,0:T(8,128)(2,1)S(1)} collective-permute-done((bf16[1024,128]{1,0:T(8,128)(2,1)S(1)}, bf16[1024,128]{1,0:T(8,128)(2,1)S(1)}, u32[]{:S(2)}, u32[]{:S(2)}) %collective-permute-start.8) | collective-permute-done | bytes 262176 | tf_op jit(solution)/shard_map/ppermute | solution.py:16
  145.0 15.6 %all_gather.23 = bf16[256,128]{1,0:T(8,128)(2,1)S(1)} all-gather(bf16[32,128]{1,0:T(8,128)(2,1)S(1)} %fusion.10), channel_id=1, replica_groups=mesh['leaf'=64,'sec'=8] {'sec'}, dimensions={0}, use_global_device_ids=true | all-gather | bytes 73728 | tf_op jit(solution)/shard_map/all_gather | solution.py:31
  168.0 5.3 collective-permute-done.10
  175.3 5.7 %collective-permute-done.11 = bf16[1024,128]{1,0:T(8,128)(2,1)} collective-permute-done((bf16[1024,128]{1,0:T(8,128)(2,1)S(1)}, bf16[1024,128]{1,0:T(8,128)(2,1)}, u32[]{:S(2)}, u32[]{:S(2)}) %collective-permute-start.11) | collective-permute-done | bytes 262176 | tf_op jit(solution)/shard_map/ppermute | solution.py:16
  184.9 10.3 %collective-permute-done.12 = f32[1024,128]{0,1:T(8,128)S(1)} collective-permute-done((f32[1024,128]{0,1:T(8,128)S(1)}, f32[1024,128]{0,1:T(8,128)S(1)}, u32[]{:S(2)}, u32[]{:S(2)}) %collective-permute-start.12) | collective-permute-done | bytes 524320 | tf_op jit(solution)/shard_map/ppermute | solution.py:16
  197.4 6.7 %collective-permute-done.13 = f32[512,128]{0,1:T(8,128)S(1)} collective-permute-done((f32[512,128]{0,1:T(8,128)S(1)}, f32[512,128]{0,1:T(8,128)S(1)}, u32[]{:S(2)}, u32[]{:S(2)}) %collective-permute-start.13) | collective-permute-done | bytes 262176 | tf_op jit(solution)/shard_map/ppermute | solution.py:16
  206.1 3.8 collective-permute-done.14
  210.8 41.2 %reduce-scatter.19.cloned.1.call-done = f32[32,128]{1,0:T(8,128)} async-done(((f32[256,128]{1,0:T(8,128)}), f32[32,128]{1,0:T(8,128)}) %reduce-scatter.19.cloned.1.call-update) | async-done | bytes 16400
  255.3 10.9 %collective-permute-done.15 = f32[1024,128]{0,1:T(8,128)S(1)} collective-permute-done((f32[1024,128]{0,1:T(8,128)S(1)}, f32[1024,128]{0,1:T(8,128)S(1)}, u32[]{:S(2)}, u32[]{:S(2)}) %collective-permute-start.15) | collective-permute-done | bytes 524320 | tf_op jit(solution)/shard_map/ppermute | solution.py:16
  269.0 6.0 %collective-permute-done.16 = f32[512,128]{0,1:T(8,128)S(1)} collective-permute-done((f32[512,128]{0,1:T(8,128)S(1)}, f32[512,128]{0,1:T(8,128)S(1)}, u32[]{:S(2)}, u32[]{:S(2)}) %collective-permute-start.16) | collective-permute-done | bytes 262176 | tf_op jit(solution)/shard_map/ppermute | solution.py:16
  277.0 3.8 collective-permute-done.17
  281.7 43.9 %reduce-scatter.21.cloned.1.call-done = f32[32,128]{1,0:T(8,128)} async-done(((f32[256,128]{1,0:T(8,128)}), f32[32,128]{1,0:T(8,128)}) %reduce-scatter.21.cloned.1.call-update) | async-done | bytes 16400 | tf_op jit(solution)/shard_map/reduce_scatter | solution.py:50
  326.7 3.7 collective-permute-start.18
  330.4 5.3 collective-permute-done.18
  337.7 3.8 collective-permute-done.19
  342.3 41.3 %reduce-scatter.23.cloned.1.call-done = f32[32,128]{1,0:T(8,128)} async-done(((f32[256,128]{1,0:T(8,128)}), f32[32,128]{1,0:T(8,128)}) %reduce-scatter.23.cloned.1.call-update) | async-done | bytes 16400
  384.7 3.9 collective-permute-start.20
  388.6 5.2 collective-permute-done.20
  395.9 3.8 collective-permute-done.21
  400.5 41.4 %reduce-scatter.25.cloned.1.call-done = f32[32,128]{1,0:T(8,128)} async-done(((f32[256,128]{1,0:T(8,128)}), f32[32,128]{1,0:T(8,128)}) %reduce-scatter.25.cloned.1.call-update) | async-done | bytes 16400 | tf_op jit(solution)/shard_map/reduce_scatter | solution.py:50
  445.1 3.6 collective-permute-done.22
  449.8 38.3 %reduce-scatter.27.cloned.1.call-done = f32[32,128]{1,0:T(8,128)} async-done(((f32[256,128]{1,0:T(8,128)}), f32[32,128]{1,0:T(8,128)}) %reduce-scatter.27.cloned.1.call-update) | async-done | bytes 16400
  491.3 3.5 collective-permute-done.23
  496.3 37.8 %reduce-scatter.29.cloned.1.call-done = f32[32,128]{1,0:T(8,128)} async-done(((f32[256,128]{1,0:T(8,128)}), f32[32,128]{1,0:T(8,128)}) %reduce-scatter.29.cloned.1.call-update) | async-done | bytes 16400
  (126 shorter events, 85.5 us)
Async XLA Ops:
  7.2 244.8 %reduce-scatter.19.cloned.1.call-start = ((), (), s32[]{:S(2)}) async-start(), calls=%async_computation.6 | async-start | bytes 147456
  29.6 5.4 collective-permute-start
  48.7 5.4 collective-permute-start.1
  68.5 5.4 collective-permute-start.2
  74.0 7.2 %collective-permute-start.3 = (bf16[512,128]{1,0:T(8,128)(2,1)S(1)}, bf16[512,128]{1,0:T(8,128)(2,1)S(1)}, u32[]{:S(2)}, u32[]{:S(2)}) collective-permute-start(bf16[512,128]{1,0:T(8,128)(2,1)S(1)} %maximum_select_fusion.15), channel_id=1, source_target_pairs={{0,16},{16,0},{8,24},{24,8},{32,48},{48,32},{40,56},{56,40},{64,80... | collective-permute-start | bytes 393224 | tf_op jit(solution)/shard_map/ppermute | solution.py:16
  96.1 5.4 collective-permute-start.4
  101.5 7.2 %collective-permute-start.5 = (bf16[512,128]{1,0:T(8,128)(2,1)S(1)}, bf16[512,128]{1,0:T(8,128)(2,1)S(1)}, u32[]{:S(2)}, u32[]{:S(2)}) collective-permute-start(bf16[512,128]{1,0:T(8,128)(2,1)S(1)} %maximum_select_fusion.16), channel_id=1, source_target_pairs={{0,16},{16,0},{8,24},{24,8},{32,48},{48,32},{40,56},{56,40},{64,80... | collective-permute-start | bytes 393224 | tf_op jit(solution)/shard_map/ppermute | solution.py:16
  109.7 71.3 %copy-start.5 = (bf16[3,32,128]{2,1,0:T(8,128)(2,1)S(1)}, bf16[3,32,128]{2,1,0:T(8,128)(2,1)}, u32[]{:S(2)}) copy-start(bf16[3,32,128]{2,1,0:T(8,128)(2,1)} %param.18) | copy-start | bytes 73732
  124.5 5.4 collective-permute-start.6
  129.9 7.2 %collective-permute-start.7 = (bf16[512,128]{1,0:T(8,128)(2,1)S(1)}, bf16[512,128]{1,0:T(8,128)(2,1)S(1)}, u32[]{:S(2)}, u32[]{:S(2)}) collective-permute-start(bf16[512,128]{1,0:T(8,128)(2,1)S(1)} %maximum_select_fusion.17), channel_id=1, source_target_pairs={{0,16},{16,0},{8,24},{24,8},{32,48},{48,32},{40,56},{56,40},{64,80... | collective-permute-start | bytes 393224 | tf_op jit(solution)/shard_map/ppermute | solution.py:16
  137.2 7.5 %collective-permute-start.8 = (bf16[1024,128]{1,0:T(8,128)(2,1)S(1)}, bf16[1024,128]{1,0:T(8,128)(2,1)S(1)}, u32[]{:S(2)}, u32[]{:S(2)}) collective-permute-start(bf16[1024,128]{1,0:T(8,128)(2,1)S(1)} %maximum_select_fusion.9), channel_id=1, source_target_pairs={{0,32},{32,0},{8,40},{40,8},{16,48},{48,16},{24,56},{56,24},{64,96... | collective-permute-start | bytes 786440 | tf_op jit(solution)/shard_map/ppermute | solution.py:16
  160.6 5.4 collective-permute-start.9
  166.1 7.2 %collective-permute-start.10 = (bf16[512,128]{1,0:T(8,128)(2,1)S(1)}, bf16[512,128]{1,0:T(8,128)(2,1)S(1)}, u32[]{:S(2)}, u32[]{:S(2)}) collective-permute-start(bf16[512,128]{1,0:T(8,128)(2,1)S(1)} %maximum_select_fusion.18), channel_id=1, source_target_pairs={{0,16},{16,0},{8,24},{24,8},{32,48},{48,32},{40,56},{56,40},{64,80... | collective-permute-start | bytes 393224 | tf_op jit(solution)/shard_map/ppermute | solution.py:16
  173.4 7.6 %collective-permute-start.11 = (bf16[1024,128]{1,0:T(8,128)(2,1)S(1)}, bf16[1024,128]{1,0:T(8,128)(2,1)}, u32[]{:S(2)}, u32[]{:S(2)}) collective-permute-start(bf16[1024,128]{1,0:T(8,128)(2,1)S(1)} %maximum_select_fusion.10), channel_id=1, source_target_pairs={{0,32},{32,0},{8,40},{40,8},{16,48},{48,16},{24,56},{56,24},{64,96... | collective-permute-start | bytes 786440 | tf_op jit(solution)/shard_map/ppermute | solution.py:16
  183.0 12.2 %collective-permute-start.12 = (f32[1024,128]{0,1:T(8,128)S(1)}, f32[1024,128]{0,1:T(8,128)S(1)}, u32[]{:S(2)}, u32[]{:S(2)}) collective-permute-start(f32[1024,128]{0,1:T(8,128)S(1)} %slice_select_fusion.1), channel_id=1, source_target_pairs={{0,32},{32,0},{8,40},{40,8},{16,48},{48,16},{24,56},{56,24},{64,96... | collective-permute-start | bytes 1572872 | tf_op jit(solution)/shard_map/ppermute | solution.py:16
  195.4 8.8 %collective-permute-start.13 = (f32[512,128]{0,1:T(8,128)S(1)}, f32[512,128]{0,1:T(8,128)S(1)}, u32[]{:S(2)}, u32[]{:S(2)}) collective-permute-start(f32[512,128]{0,1:T(8,128)S(1)} %slice_select_fusion.5), channel_id=1, source_target_pairs={{0,16},{16,0},{8,24},{24,8},{32,48},{48,32},{40,56},{56,40},{64,80... | collective-permute-start | bytes 786440 | tf_op jit(solution)/shard_map/ppermute | solution.py:16
  204.2 5.7 %collective-permute-start.14 = (f32[256,128]{0,1:T(8,128)S(1)}, f32[256,128]{0,1:T(8,128)S(1)}, u32[]{:S(2)}, u32[]{:S(2)}) collective-permute-start(f32[256,128]{0,1:T(8,128)S(1)} %slice_select_fusion.11), channel_id=1, source_target_pairs={{0,8},{8,0},{16,24},{24,16},{32,40},{40,32},{48,56},{56,48},{64,72... | collective-permute-start | bytes 393224 | tf_op jit(solution)/shard_map/ppermute | solution.py:16
  210.7 114.9 %reduce-scatter.21.cloned.1.call-start = ((), (), s32[]{:S(2)}) async-start(), calls=%async_computation.7 | async-start | bytes 147456 | tf_op jit(solution)/shard_map/reduce_scatter | solution.py:50
  253.2 13.1 %collective-permute-start.15 = (f32[1024,128]{0,1:T(8,128)S(1)}, f32[1024,128]{0,1:T(8,128)S(1)}, u32[]{:S(2)}, u32[]{:S(2)}) collective-permute-start(f32[1024,128]{0,1:T(8,128)S(1)} %slice_select_fusion), channel_id=1, source_target_pairs={{0,32},{32,0},{8,40},{40,8},{16,48},{48,16},{24,56},{56,24},{64,96... | collective-permute-start | bytes 1572872 | tf_op jit(solution)/shard_map/ppermute | solution.py:16
  266.4 8.6 %collective-permute-start.16 = (f32[512,128]{0,1:T(8,128)S(1)}, f32[512,128]{0,1:T(8,128)S(1)}, u32[]{:S(2)}, u32[]{:S(2)}) collective-permute-start(f32[512,128]{0,1:T(8,128)S(1)} %slice_select_fusion.4), channel_id=1, source_target_pairs={{0,16},{16,0},{8,24},{24,8},{32,48},{48,32},{40,56},{56,40},{64,80... | collective-permute-start | bytes 786440 | tf_op jit(solution)/shard_map/ppermute | solution.py:16
  275.1 5.7 %collective-permute-start.17 = (f32[256,128]{0,1:T(8,128)S(1)}, f32[256,128]{0,1:T(8,128)S(1)}, u32[]{:S(2)}, u32[]{:S(2)}) collective-permute-start(f32[256,128]{0,1:T(8,128)S(1)} %slice_select_fusion.10), channel_id=1, source_target_pairs={{0,8},{8,0},{16,24},{24,16},{32,40},{40,32},{48,56},{56,48},{64,72... | collective-permute-start | bytes 393224 | tf_op jit(solution)/shard_map/ppermute | solution.py:16
  281.6 102.0 %reduce-scatter.23.cloned.1.call-start = ((), (), s32[]{:S(2)}) async-start(), calls=%async_computation.8 | async-start | bytes 147456
  326.7 9.0 %collective-permute-start.18 = (f32[512,128]{0,1:T(8,128)S(1)}, f32[512,128]{0,1:T(8,128)S(1)}, u32[]{:S(2)}, u32[]{:S(2)}) collective-permute-start(f32[512,128]{0,1:T(8,128)S(1)} %slice_select_fusion.3), channel_id=1, source_target_pairs={{0,16},{16,0},{8,24},{24,8},{32,48},{48,32},{40,56},{56,40},{64,80... | collective-permute-start | bytes 786440 | tf_op jit(solution)/shard_map/ppermute | solution.py:16
  335.8 5.7 %collective-permute-start.19 = (f32[256,128]{0,1:T(8,128)S(1)}, f32[256,128]{0,1:T(8,128)S(1)}, u32[]{:S(2)}, u32[]{:S(2)}) collective-permute-start(f32[256,128]{0,1:T(8,128)S(1)} %slice_select_fusion.9), channel_id=1, source_target_pairs={{0,8},{8,0},{16,24},{24,16},{32,40},{40,32},{48,56},{56,48},{64,72... | collective-permute-start | bytes 393224 | tf_op jit(solution)/shard_map/ppermute | solution.py:16
  342.3 99.6 %reduce-scatter.25.cloned.1.call-start = ((), (), s32[]{:S(2)}) async-start(), calls=%async_computation.9 | async-start | bytes 147456 | tf_op jit(solution)/shard_map/reduce_scatter | solution.py:50
  384.7 65.0 %copy-start.7 = (bf16[1024]{0:T(1024)(128)(2,1)S(1)}, bf16[1024]{0:T(1024)(128)(2,1)}, u32[]{:S(2)}) copy-start(bf16[1024]{0:T(1024)(128)(2,1)} %param.14) | copy-start | bytes 6148
  384.7 9.1 %collective-permute-start.20 = (f32[512,128]{0,1:T(8,128)S(1)}, f32[512,128]{0,1:T(8,128)S(1)}, u32[]{:S(2)}, u32[]{:S(2)}) collective-permute-start(f32[512,128]{0,1:T(8,128)S(1)} %slice_select_fusion.2), channel_id=1, source_target_pairs={{0,16},{16,0},{8,24},{24,8},{32,48},{48,32},{40,56},{56,40},{64,80... | collective-permute-start | bytes 786440 | tf_op jit(solution)/shard_map/ppermute | solution.py:16
  393.9 5.7 %collective-permute-start.21 = (f32[256,128]{0,1:T(8,128)S(1)}, f32[256,128]{0,1:T(8,128)S(1)}, u32[]{:S(2)}, u32[]{:S(2)}) collective-permute-start(f32[256,128]{0,1:T(8,128)S(1)} %slice_select_fusion.8), channel_id=1, source_target_pairs={{0,8},{8,0},{16,24},{24,16},{32,40},{40,32},{48,56},{56,48},{64,72... | collective-permute-start | bytes 393224 | tf_op jit(solution)/shard_map/ppermute | solution.py:16
  400.5 87.6 %reduce-scatter.27.cloned.1.call-start = ((), (), s32[]{:S(2)}) async-start(), calls=%async_computation.10 | async-start | bytes 147456
  442.9 5.7 %collective-permute-start.22 = (f32[256,128]{0,1:T(8,128)S(1)}, f32[256,128]{0,1:T(8,128)S(1)}, u32[]{:S(2)}, u32[]{:S(2)}) collective-permute-start(f32[256,128]{0,1:T(8,128)S(1)} %slice_select_fusion.7), channel_id=1, source_target_pairs={{0,8},{8,0},{16,24},{24,16},{32,40},{40,32},{48,56},{56,48},{64,72... | collective-permute-start | bytes 393224 | tf_op jit(solution)/shard_map/ppermute | solution.py:16
  449.4 84.7 %reduce-scatter.29.cloned.1.call-start = ((), (), s32[]{:S(2)}) async-start(), calls=%async_computation.11 | async-start | bytes 147456
  489.1 5.7 %collective-permute-start.23 = (f32[256,128]{0,1:T(8,128)S(1)}, f32[256,128]{0,1:T(8,128)S(1)}, u32[]{:S(2)}, u32[]{:S(2)}) collective-permute-start(f32[256,128]{0,1:T(8,128)S(1)} %slice_select_fusion.6), channel_id=1, source_target_pairs={{0,8},{8,0},{16,24},{24,16},{32,40},{40,32},{48,56},{56,48},{64,72... | collective-permute-start | bytes 393224 | tf_op jit(solution)/shard_map/ppermute | solution.py:16
  (7 other events, 246.7 us)
Sparse Core Ops, SparseCore 0:
  210.8 41.1 reduce-scatter.18
  281.8 43.7 reduce-scatter.20
  342.4 41.1 reduce-scatter.22
  400.6 41.2 reduce-scatter.24
  449.6 38.4 reduce-scatter.26
  495.7 38.3 reduce-scatter.28
where the time goes:
time: 545 us; the launch traced here: 543 us
  waiting for transfers between devices  364 us (67%)
  blocking collectives  91.6 us (17%)
  starting transfers between devices  51.5 us (9%)
  between operations  15.5 us (3%)
  local copies, waits for them, and re-layouts  10.3 us (2%)
  matrix products  8.35 us (2%)
    unnamed x10, waiting for transfers between devices  159 us
    ppermute x24, waiting for transfers between devices, from_partner(): return lax.ppermute(block, axis, route)  120 us
    all_gather x6, blocking collectives, group_gather(): block = lax.all_gather(piece, 'sec', axis=0, tiled=True)  91.6 us
    reduce_scatter x2, waiting for transfers between devices, group_reduce(): return lax.psum_scatter(reduced, 'sec', scatter_dimension=0, tiled=True)  85.3 us
    ppermute x24, starting transfers between devices, from_partner(): return lax.ppermute(block, axis, route)  51.3 us
  transfers between devices with their start and end apart: 30, of which 30 were waited for; matrix products, arithmetic and copies ran while one was open for 0% of the time, Pallas kernels for 0%

commit v1 on v0

v1 whole, which is shorter than its diff:
```python
import functools

import jax
import jax.numpy as jnp
from jax import lax
from jax.experimental import pallas as pl
from jax.experimental.pallas import tpu as pltpu
from jax.sharding import PartitionSpec as P

MESH = pl.DeviceIdType.MESH
BLOCK = 128
BF = jnp.bfloat16
F32 = jnp.float32
ROWS = 1024
SEP = 32
SECS = 8
SPAN = SECS * SEP
SAMP = 16
NEAR = {1: (1,), 2: (1, 3, 2), 3: (1, 3, 4, 2, 5, 7, 6)}
SEC_PEERS = (6, 4, 7, 5, 2, 3, 1)
X_PEERS = (2, 6, 4)


def dot(a, b, ca, cb):
    return lax.dot_general(a, b, (((ca,), (cb,)), ((), ())), preferred_element_type=F32)


def kernel(
    leaf_inv, blocks, rhs, noise, dev, sep_inv, sep_panel, sep_rhs, sep_noise, sep_dev,
    out, sep_out,
    d_v, rhs_v, noise_v, w_v, x_v, scale_v,
    p1, q1, p2, q2, p3, q3,
    c1_src, c1_buf, rn_src, rn_buf, item_v, f_buf, b_src, b_buf, o_src, o_buf, s_src, s_buf,
    ld_sem, c1_s, c1_r, rn_s, rn_r, own_sem, x_r, d_r, mat_s, f_s, f_r, b_s, b_r, o_s, o_r, s_s, s_r,
):
    leaf = lax.axis_index("leaf")
    sec = lax.axis_index("sec")

    def at(leaf_mask, sec_mask):
        return (leaf ^ leaf_mask, sec ^ sec_mask)

    def send(src, dst, send_sem, recv_sem, leaf_mask, sec_mask):
        pltpu.make_async_remote_copy(
            src_ref=src, dst_ref=dst, send_sem=send_sem, recv_sem=recv_sem,
            device_id=at(leaf_mask, sec_mask), device_id_type=MESH,
        ).start()

    def wait(ref, sem):
        pltpu.make_async_copy(ref, ref, sem).wait()

    barrier = pltpu.get_barrier_semaphore()
    peers = [(1, m) for m in SEC_PEERS] + [(0, m) for m in SEC_PEERS] + [(m, 0) for m in reversed(NEAR[3])]
    for leaf_mask, sec_mask in peers:
        pl.semaphore_signal(barrier, inc=1, device_id=at(leaf_mask, sec_mask), device_id_type=MESH)

    edge = ROWS - SEP
    loads = [
        (rhs, rhs_v),
        (leaf_inv.at[pl.ds(edge, SEP)], d_v.at[pl.ds(edge, SEP)]),
        (leaf_inv.at[pl.ds(0, edge)], d_v.at[pl.ds(0, edge)]),
        (noise, noise_v),
    ]
    for i, (src, dst) in enumerate(loads):
        pltpu.make_async_copy(src, dst, ld_sem.at[i]).start()

    def loaded(i):
        pltpu.make_async_copy(loads[i][0], loads[i][1], ld_sem.at[i]).wait()

    place = lax.broadcasted_iota(jnp.int32, (128, 128), 0) + 32 * (sec & 3)
    lane = lax.broadcasted_iota(jnp.int32, (128, 128), 1)
    turn = jnp.where(lane == (place & 127), F32(1), F32(0)).astype(BF)
    turn_edge = turn[:SEP]
    first = jnp.concatenate([sep_rhs[0], sep_rhs[1], sep_rhs[2], sep_noise[0]], axis=0)
    second = jnp.concatenate([sep_noise[1], sep_noise[2]], axis=0)
    rn_src[:, :128] = dot(first, turn, 0, 0).astype(BF)
    rn_src[:, 128:] = dot(second, turn[: 2 * SEP], 0, 0).astype(BF)
    mine = pl.ds(pl.multiple_of(sec * SAMP, SAMP), SAMP)
    rn_buf[sec] = rn_src[mine, :]

    dead = ROWS - blocks[0, 0] * BLOCK
    row_id = lax.broadcasted_iota(jnp.int32, (ROWS, 128), 0)
    loaded(0)
    rhs_v[...] = jnp.where(row_id >= dead, rhs_v[...].astype(F32), F32(0)).astype(BF)
    loaded(1)
    live_edge = lax.broadcasted_iota(jnp.int32, (SEP, 128), 0) + edge >= dead
    y_edge = dot(d_v[pl.ds(edge, SEP), :], rhs_v[...], 1, 0)
    y_edge = jnp.where(live_edge, y_edge, F32(0)).astype(BF)
    c1_src[...] = dot(y_edge, turn_edge, 0, 0).astype(BF)
    c1_buf[sec] = c1_src[mine, :]

    pl.semaphore_wait(barrier, len(peers))

    def part(ref, sec_mask):
        return ref.at[pl.ds(pl.multiple_of((sec ^ sec_mask) * SAMP, SAMP), SAMP)]

    for leaf_mask in (1, 0):
        for m in SEC_PEERS + ((0,) if leaf_mask else ()):
            send(part(c1_src, m), c1_buf.at[SECS * leaf_mask + sec], c1_s, c1_r, leaf_mask, m)
    for m in SEC_PEERS:
        send(part(rn_src, m), rn_buf.at[sec], rn_s, rn_r, 0, m)

    chunks = []
    for height, (p, q) in enumerate(((p1, q1), (p2, q2), (p3, q3)), 1):
        cols = pl.ds((2**height - 2) * SPAN, 2**height * SPAN)
        chunks += [(sep_panel.at[:, cols], p), (sep_inv.at[:, cols], q)]

    def rows_of(sec_mask):
        return pl.ds(pl.multiple_of((sec ^ sec_mask) * SEP, SEP), SEP)

    for j, (src, dst) in enumerate(chunks):
        for i, m in enumerate(X_PEERS):
            send(src, dst.at[rows_of(0)], mat_s.at[j], x_r.at[j, i], 0, m)
        send(src, dst.at[rows_of(0)], mat_s.at[j], d_r.at[j], 0, 1)
        pltpu.make_async_copy(src, dst.at[rows_of(0)], own_sem.at[j]).start()

    def forward(j):
        dst = chunks[j][1]
        for i, m in enumerate(X_PEERS):
            block = dst.at[rows_of(m)]
            wait(block, x_r.at[j, i])
            send(block, block, mat_s.at[j], d_r.at[j], 0, 1)

    def ready(j):
        src, dst = chunks[j]
        pltpu.make_async_copy(src, dst.at[rows_of(0)], own_sem.at[j]).wait()
        wait(dst.at[pl.ds(0, 4 * SEP)], d_r.at[j])
        return dst

    loaded(2)
    loaded(3)
    for t in range(4):
        rows = pl.ds(256 * t, 256)
        live = lax.broadcasted_iota(jnp.int32, (256, 128), 0) + 256 * t
        y = dot(d_v[rows, :], rhs_v[...], 1, 0).astype(BF).astype(F32)
        w = y + noise_v[rows, :].astype(F32)
        w_v[rows, :] = jnp.where((live >= dead) & (live < edge), w, F32(0)).astype(BF)
    for t in range(4):
        rows = pl.ds(256 * t, 256)
        x_v[rows, :] = dot(d_v[:, rows], w_v[...], 0, 0)
    eye = lax.broadcasted_iota(jnp.int32, (128, 128), 0) == lane
    for t in range(8):
        rows = pl.ds(128 * t, 128)
        diag = jnp.where(eye, jnp.broadcast_to(dev[t : t + 1, :].astype(F32), (128, 128)), F32(0))
        live = lax.broadcasted_iota(jnp.int32, (128, 128), 0) + 128 * t >= dead
        scale = jnp.broadcast_to(jnp.sum(diag, axis=1, keepdims=True), (128, 128))
        scale_v[rows, :] = jnp.where(live, scale, F32(0))

    wait(rn_buf.at[pl.ds(0, 7)], rn_r)
    group = lax.broadcasted_iota(jnp.int32, (SAMP, 128), 1) // SEP
    for item in range(6):
        tile, j = item // 4, item % 4
        for half in range(2):
            got = jnp.zeros((SAMP, 128), F32)
            for s in range(4):
                piece = rn_buf[4 * half + s, :, 128 * tile : 128 * tile + 128].astype(F32)
                got = jnp.where(group == (j + s) % 4, piece, got)
            if j:
                got = pltpu.roll(got, 128 - SEP * j, 1)
            item_v[item, :, 128 * half : 128 * half + 128] = got

    forward(0)
    wait(c1_buf.at[pl.ds(0, 15)], c1_r)

    def cols_of(height, mask):
        return pl.ds(pl.multiple_of(((leaf ^ mask) & (2**height - 1)) * SPAN, SPAN), SPAN)

    def publish(e, height, value):
        f_buf[e, 0] = value
        for m in reversed(NEAR[height]):
            send(f_buf.at[e, 0], f_buf.at[e, m], f_s.at[e], f_r.at[e, m], m, 0)

    def gathered_product(e, height, j):
        matrix = ready(j)
        total = dot(f_buf[e, 0], matrix[:, cols_of(height, 0)], 1, 1)
        for m in NEAR[height]:
            wait(f_buf.at[e, m], f_r.at[e, m])
            total += dot(f_buf[e, m], matrix[:, cols_of(height, m)], 1, 1)
        return total

    matrix = ready(0)
    total = jnp.zeros((SAMP, SPAN), F32)
    for leaf_mask in range(2):
        halves = []
        for half in range(2):
            pieces = [c1_buf[SECS * leaf_mask + 4 * half + s].astype(F32) for s in range(4)]
            halves.append((pieces[0] + pieces[1]) + (pieces[2] + pieces[3]))
        child = jnp.concatenate(halves, axis=1).astype(BF)
        total += dot(child, matrix[:, cols_of(1, leaf_mask)], 1, 1)
    solved = []
    for height in range(1, 4):
        if height > 1:
            total = gathered_product(2 * height - 3, height, 2 * height - 2)
        publish(2 * height - 2, height, (item_v[height - 1] - total).astype(BF))
        forward(2 * height - 1)
        y = gathered_product(2 * height - 2, height, 2 * height - 1).astype(BF)
        solved.append(y)
        if height < 3:
            publish(2 * height - 1, height + 1, y)
            forward(2 * height)

    def scattered_product(e, height, j, vector):
        matrix = chunks[j][1]
        for m in reversed(NEAR[height]):
            b_src[e, m] = dot(vector, matrix[:, cols_of(height, m)], 1, 0).astype(BF)
            send(b_src.at[e, m], b_buf.at[e, m], b_s.at[e], b_r.at[e, m], m, 0)
        total = dot(vector, matrix[:, cols_of(height, 0)], 1, 0)
        for m in NEAR[height]:
            wait(b_buf.at[e, m], b_r.at[e, m])
            total += b_buf[e, m].astype(F32)
        return total

    def half_of(ref, mask):
        start = pl.multiple_of(((sec ^ mask) >> 2) * 128, 128)
        return ref.at[:, pl.ds(start, 128)]

    def give_back(level, value):
        for half in range(2):
            o_src[level, half] = value[:, 128 * half : 128 * half + 128]
        o_buf[level, sec] = o_src[level, sec >> 2]
        for m in SEC_PEERS:
            send(o_src.at[level, (sec ^ m) >> 2], o_buf.at[level, sec], o_s.at[level], o_r.at[level], 0, m)

    def write_sample(level):
        wait(o_buf.at[level, pl.ds(0, 7)], o_r.at[level])
        flat = o_buf[level].reshape(128, 128)
        mine = dot(turn_edge, flat, 1, 1)
        row = jnp.broadcast_to(sep_dev[level : level + 1, :].astype(F32), (SEP, SEP))
        small = lax.broadcasted_iota(jnp.int32, (SEP, SEP), 0) == lax.broadcasted_iota(jnp.int32, (SEP, SEP), 1)
        scale = jnp.sum(jnp.where(small, row, F32(0)), axis=1, keepdims=True)
        sep_out[level] = (jnp.broadcast_to(scale, (SEP, 128)) * mine).astype(BF)

    minus = None
    e = 0
    for height in range(3, 0, -1):
        summed = solved[height - 1].astype(F32) + item_v[2 + height]
        if minus is not None:
            summed = summed - minus
        backed = scattered_product(e, height, 2 * height - 1, summed.astype(BF)).astype(BF)
        e += 1
        if height > 1:
            minus = scattered_product(e, height, 2 * height - 2, backed)
            e += 1
            give_back(height - 1, backed)
    for leaf_mask in (1, 0):
        pushed = dot(backed, p1[:, cols_of(1, leaf_mask)], 1, 0).astype(BF)
        for half in range(2):
            s_src[leaf_mask, half] = pushed[:, 128 * half : 128 * half + 128]
        for m in SEC_PEERS + ((0,) if leaf_mask else ()):
            send(s_src.at[leaf_mask, (sec ^ m) >> 2], s_buf.at[SECS * leaf_mask + sec], s_s, s_r, leaf_mask, m)
    s_buf[sec] = s_src[0, sec >> 2]
    give_back(0, backed)
    write_sample(2)
    write_sample(1)
    wait(s_buf.at[pl.ds(0, 15)], s_r)
    s0 = dot(turn_edge, s_buf[0:8].reshape(128, 128), 1, 1) + dot(turn_edge, s_buf[8:16].reshape(128, 128), 1, 1)
    w_edge = y_edge.astype(F32) + noise_v[pl.ds(edge, SEP), :].astype(F32) - s0
    w_edge = jnp.where(live_edge, w_edge, F32(0)).astype(BF)
    for t in range(4):
        rows = pl.ds(256 * t, 256)
        x = x_v[rows, :] + dot(d_v[pl.ds(edge, SEP), rows], w_edge, 0, 0)
        out[rows, :] = (scale_v[rows, :] * x).astype(BF)
    write_sample(0)

    wait(c1_buf.at[pl.ds(0, 15)], c1_s)
    wait(rn_buf.at[pl.ds(0, 7)], rn_s)
    for j, (_, dst) in enumerate(chunks):
        wait(dst.at[pl.ds(0, 7 * SEP)], mat_s.at[j])
    for e, height in enumerate((1, 2, 2, 3, 3)):
        wait(f_buf.at[e, pl.ds(0, 2**height - 1)], f_s.at[e])
    for e, height in enumerate((3, 3, 2, 2, 1)):
        wait(b_buf.at[e, pl.ds(0, 2**height - 1)], b_s.at[e])
    for level in range(3):
        wait(o_buf.at[level, pl.ds(0, 7)], o_s.at[level])
    wait(s_buf.at[pl.ds(0, 15)], s_s)


def on_device(leaf_inv, blocks, rhs, noise, dev, sep_inv, sep_panel, sep_rhs, sep_noise, sep_dev):
    dma = pltpu.SemaphoreType.DMA
    vmem = pltpu.VMEM
    anywhere = pl.BlockSpec(memory_space=pl.ANY)
    held = pl.BlockSpec(memory_space=vmem)
    scratch = [
        vmem((ROWS, ROWS), BF), vmem((ROWS, 128), BF), vmem((ROWS, 128), BF), vmem((ROWS, 128), BF),
        vmem((ROWS, 128), F32), vmem((ROWS, 128), F32),
    ]
    for height in (1, 2, 3):
        scratch += [vmem((SPAN, 2**height * SPAN), BF)] * 2
    scratch += [
        vmem((128, 128), BF), vmem((2 * SECS, SAMP, 128), BF),
        vmem((128, 256), BF), vmem((SECS, SAMP, 256), BF), vmem((6, SAMP, SPAN), F32),
        vmem((5, 8, SAMP, SPAN), BF), vmem((5, 8, SAMP, SPAN), BF), vmem((5, 8, SAMP, SPAN), BF),
        vmem((3, 2, SAMP, 128), BF), vmem((3, SECS, SAMP, 128), BF),
        vmem((2, 2, SAMP, 128), BF), vmem((2 * SECS, SAMP, 128), BF),
    ]
    scratch += [
        dma((4,)), dma, dma, dma, dma, dma((6,)), dma((6, 3)), dma((6,)), dma((6,)),
        dma((5,)), dma((5, 8)), dma((5,)), dma((5, 8)), dma((3,)), dma((3,)), dma, dma,
    ]
    return pl.pallas_call(
        kernel,
        out_shape=(
            jax.ShapeDtypeStruct(rhs.shape, BF),
            jax.ShapeDtypeStruct(sep_rhs.shape, BF),
        ),
        in_specs=[
            anywhere, pl.BlockSpec(memory_space=pltpu.SMEM), anywhere, anywhere, held,
            anywhere, anywhere, held, held, held,
        ],
        out_specs=(held, held),
        scratch_shapes=scratch,
        compiler_params=pltpu.CompilerParams(
            collective_id=0, has_side_effects=True, vmem_limit_bytes=40 * 2**20
        ),
    )(leaf_inv, blocks, rhs, noise, dev.reshape(8, 128), sep_inv, sep_panel, sep_rhs, sep_noise, sep_dev)


def solution(mesh):
    both = ("leaf", "sec")
    in_specs = (
        P(both, None), P("leaf", "sec"), P(both, None), P(both, None), P(both),
        P(both, None), P(both, None), P(None, both, None), P(None, both, None), P(None, both),
    )
    return jax.shard_map(
        on_device, mesh=mesh, in_specs=in_specs,
        out_specs=(P(both, None), P(None, both, None)), check_vma=False,
    )
```

time: 545 us -> 69.8 us (0.13)
  waiting for transfers between devices: 364 us -> 0 us
  blocking collectives: 91.6 us -> 0 us
  Pallas kernels: 0 us -> 58.5 us
  starting transfers between devices: 51.5 us -> 0 us
  between operations: 15.5 us -> 1.3 us
  matrix products: 8.35 us -> 0 us
    unnamed x10 -> x0, waiting for transfers between devices: 159 us -> none
    ppermute x24 -> x0, waiting for transfers between devices: 120 us -> none  [from_partner(): return lax.ppermute(block, axis, route)]
    all_gather x6 -> x0, blocking collectives: 91.6 us -> none  [group_gather(): block = lax.all_gather(piece, 'sec', axis=0, tiled=True)]
    reduce_scatter x2 -> x0, waiting for transfers between devices: 85.3 us -> none  [group_reduce(): return lax.psum_scatter(reduced, 'sec', scatter_dimension=0, tiled=True)]
    pallas_call x0 -> x1, Pallas kernels: none -> 58.5 us  [on_device(): pl.pallas_call(kernel, out_shape=(jax.ShapeDtypeStruct(rhs.shape, BF), ja...]
    ppermute x24 -> x0, starting transfers between devices: 51.3 us -> none  [from_partner(): return lax.ppermute(block, axis, route)]
    dot_general x13 -> x0, matrix products: 8.35 us -> none  [the longest x7 5.01 us: transposed_product(): lax.dot_general(matrix, vector, (((0,), (0,)), ((), ())), preferred_eleme...]
  transfers between devices with their start and end apart: 30 -> 0, of which waited for: 30 -> 0; matrix products, arithmetic and copies ran while one was open for 0% -> 0% of each run, Pallas kernels for 0% -> 0%
where the time goes in v1:
time: 69.8 us; the launch traced here: 69.3 us
  Pallas kernels  58.5 us (84%)
  local copies, waits for them, and re-layouts  9.5 us (14%)
  between operations  1.3 us (2%)
    pallas_call x1, Pallas kernels, on_device(): pl.pallas_call(kernel, out_shape=(jax.ShapeDtypeStruct(rhs.shape, BF), ja...  58.5 us
    unnamed x20, local copies, waits for them, and re-layouts  9.5 us

profile of v1, /device:TPU:1, one launch (start us, length us, event | category | flops | bytes accessed | tf_op | source)
XLA Modules:
  0.0 69.3 jit_solution(6136065932588967037)
XLA Ops:
  1.3 0.0 copy-start
  1.3 1.6 %copy-done = bf16[1024,1024]{1,0:T(8,128)(2,1)S(1)} copy-done((bf16[1024,1024]{1,0:T(8,128)(2,1)S(1)}, bf16[1024,1024]{1,0:T(8,128)(2,1)}, u32[]{:S(2)}) %copy-start) | copy-done | bytes 2097176
  2.9 0.0 copy-start.1
  2.9 0.9 %copy-done.1 = bf16[1024,128]{1,0:T(8,128)(2,1)S(1)} copy-done((bf16[1024,128]{1,0:T(8,128)(2,1)S(1)}, bf16[1024,128]{1,0:T(8,128)(2,1)}, u32[]{:S(2)}) %copy-start.1) | copy-done | bytes 262168
  3.8 0.0 copy-start.2
  3.8 0.9 %copy-done.2 = bf16[1024,128]{1,0:T(8,128)(2,1)S(1)} copy-done((bf16[1024,128]{1,0:T(8,128)(2,1)S(1)}, bf16[1024,128]{1,0:T(8,128)(2,1)}, u32[]{:S(2)}) %copy-start.2) | copy-done | bytes 262168
  4.8 0.0 copy-start.3
  4.8 0.9 %copy-done.3 = bf16[32,3584]{1,0:T(8,128)(2,1)S(1)} copy-done((bf16[32,3584]{1,0:T(8,128)(2,1)S(1)}, bf16[32,3584]{1,0:T(8,128)(2,1)}, u32[]{:S(2)}) %copy-start.3) | copy-done | bytes 229400
  5.7 0.0 copy-start.4
  5.7 0.9 %copy-done.4 = bf16[32,3584]{1,0:T(8,128)(2,1)S(1)} copy-done((bf16[32,3584]{1,0:T(8,128)(2,1)S(1)}, bf16[32,3584]{1,0:T(8,128)(2,1)}, u32[]{:S(2)}) %copy-start.4) | copy-done | bytes 229400
  6.6 0.0 copy-start.5
  6.7 0.7 %copy-done.5 = bf16[3,32,128]{2,1,0:T(8,128)(2,1)S(1)} copy-done((bf16[3,32,128]{2,1,0:T(8,128)(2,1)S(1)}, bf16[3,32,128]{2,1,0:T(8,128)(2,1)}, u32[]{:S(2)}) %copy-start.5) | copy-done | bytes 24600
  7.4 0.0 copy-start.6
  7.4 0.7 %copy-done.6 = bf16[3,32,128]{2,1,0:T(8,128)(2,1)S(1)} copy-done((bf16[3,32,128]{2,1,0:T(8,128)(2,1)S(1)}, bf16[3,32,128]{2,1,0:T(8,128)(2,1)}, u32[]{:S(2)}) %copy-start.6) | copy-done | bytes 24600
  8.1 0.0 copy-start.7
  8.1 0.7 copy-done.7
  8.8 0.0 copy-start.8
  8.8 0.7 copy-done.8
  9.5 58.5 %shard_map.113 = (bf16[1024,128]{1,0:T(8,128)(2,1)S(1)}, bf16[3,32,128]{2,1,0:T(8,128)(2,1)S(1)}) custom-call(bf16[1024,1024]{1,0:T(8,128)(2,1)S(1)} %copy-done, s32[1,1]{1,0:T(1,128)S(6)} %copy.14.blocks, bf16[1024,128]{1,0:T(8,128)(2,1)S(1)} %copy-done.1, bf16[1024,128]{1,0:T(8,128)(2,1)S(1)} %copy-done.2, bf16[8,128]{1,0:T(8,128)(2,1)S(1)} %bitcast.1, ...), custom_call_target="tpu_custom_call" | custom-call | tf_op jit(solution)/shard_map/pallas_call | solution.py:299
  68.0 0.7 %copy.15 = bf16[1024,128]{1,0:T(8,128)(2,1)} copy(bf16[1024,128]{1,0:T(8,128)(2,1)S(1)} %get-tuple-element.4) | data formatting | bytes 524288
  68.7 0.6 copy.16
Async XLA Ops:
  1.3 1.6 %copy-start = (bf16[1024,1024]{1,0:T(8,128)(2,1)S(1)}, bf16[1024,1024]{1,0:T(8,128)(2,1)}, u32[]{:S(2)}) copy-start(bf16[1024,1024]{1,0:T(8,128)(2,1)} %leaf_inv.1) | copy-start | bytes 6291460
  2.9 0.9 %copy-start.1 = (bf16[1024,128]{1,0:T(8,128)(2,1)S(1)}, bf16[1024,128]{1,0:T(8,128)(2,1)}, u32[]{:S(2)}) copy-start(bf16[1024,128]{1,0:T(8,128)(2,1)} %rhs.1) | copy-start | bytes 786436
  3.8 0.9 %copy-start.2 = (bf16[1024,128]{1,0:T(8,128)(2,1)S(1)}, bf16[1024,128]{1,0:T(8,128)(2,1)}, u32[]{:S(2)}) copy-start(bf16[1024,128]{1,0:T(8,128)(2,1)} %noise.1) | copy-start | bytes 786436
  4.8 0.9 %copy-start.3 = (bf16[32,3584]{1,0:T(8,128)(2,1)S(1)}, bf16[32,3584]{1,0:T(8,128)(2,1)}, u32[]{:S(2)}) copy-start(bf16[32,3584]{1,0:T(8,128)(2,1)} %sep_inv.1) | copy-start | bytes 688132
  5.7 0.9 %copy-start.4 = (bf16[32,3584]{1,0:T(8,128)(2,1)S(1)}, bf16[32,3584]{1,0:T(8,128)(2,1)}, u32[]{:S(2)}) copy-start(bf16[32,3584]{1,0:T(8,128)(2,1)} %sep_panel.1) | copy-start | bytes 688132
  6.6 0.7 %copy-start.5 = (bf16[3,32,128]{2,1,0:T(8,128)(2,1)S(1)}, bf16[3,32,128]{2,1,0:T(8,128)(2,1)}, u32[]{:S(2)}) copy-start(bf16[3,32,128]{2,1,0:T(8,128)(2,1)} %sep_rhs.1) | copy-start | bytes 73732
  7.4 0.7 %copy-start.6 = (bf16[3,32,128]{2,1,0:T(8,128)(2,1)S(1)}, bf16[3,32,128]{2,1,0:T(8,128)(2,1)}, u32[]{:S(2)}) copy-start(bf16[3,32,128]{2,1,0:T(8,128)(2,1)} %sep_noise.1) | copy-start | bytes 73732
  8.1 0.7 copy-start.7
  8.8 0.7 copy-start.8

commit v2 on v1

v2 whole, which is shorter than its diff:
```python
import functools

import jax
import jax.numpy as jnp
from jax import lax
from jax.experimental import pallas as pl
from jax.experimental.pallas import tpu as pltpu
from jax.sharding import PartitionSpec as P

MESH = pl.DeviceIdType.MESH
BLOCK = 128
BF = jnp.bfloat16
F32 = jnp.float32
ROWS = 1024
SEP = 32
SECS = 8
SPAN = SECS * SEP
SAMP = 16
NEAR = {1: (1,), 2: (1, 3, 2), 3: (1, 3, 4, 2, 5, 7, 6)}
SEC_PEERS = (6, 4, 7, 5, 2, 3, 1)
X_PEERS = (2, 6, 4)


def dot(a, b, ca, cb):
    return lax.dot_general(a, b, (((ca,), (cb,)), ((), ())), preferred_element_type=F32)


def kernel(
    leaf_inv, blocks_h, rhs, noise, dev_h, sep_inv, sep_panel, sep_rhs_h, sep_noise_h, sep_dev_h,
    out, sep_out,
    blocks, dev, sep_rhs, sep_noise, sep_dev, d_v, rhs_v, noise_v, w_v, x_v, scale_v,
    p1, q1, p2, q2, p3, q3,
    c1_src, c1_buf, rn_src, rn_buf, rp_buf, item_v, f_buf, b_src, b_buf, b_wide, b_near, o_src, o_buf, s_src, s_buf,
    ld_sem, c1_s, c1_r, rn_s, rn_r, rp_s, rp_r, own_sem, x_r, d_r, mat_s, f_s, f_r, b_s, b_r, w_s, w_r,
    o_s, o_r, s_s, s_r,
):
    leaf = lax.axis_index("leaf")
    sec = lax.axis_index("sec")

    def at(leaf_mask, sec_mask):
        return (leaf ^ leaf_mask, sec ^ sec_mask)

    def send(src, dst, send_sem, recv_sem, leaf_mask, sec_mask):
        pltpu.make_async_remote_copy(
            src_ref=src, dst_ref=dst, send_sem=send_sem, recv_sem=recv_sem,
            device_id=at(leaf_mask, sec_mask), device_id_type=MESH,
        ).start()

    def wait(ref, sem):
        pltpu.make_async_copy(ref, ref, sem).wait()

    barrier = pltpu.get_barrier_semaphore()
    peers = [(1, m) for m in SEC_PEERS] + [(0, m) for m in SEC_PEERS] + [(m, 0) for m in reversed(NEAR[3])]
    for leaf_mask, sec_mask in peers:
        pl.semaphore_signal(barrier, inc=1, device_id=at(leaf_mask, sec_mask), device_id_type=MESH)

    edge = ROWS - SEP
    loads = [
        (rhs, rhs_v),
        (leaf_inv.at[pl.ds(edge, SEP)], d_v.at[pl.ds(edge, SEP)]),
        (leaf_inv.at[pl.ds(0, edge)], d_v.at[pl.ds(0, edge)]),
        (noise, noise_v),
        (sep_rhs_h, sep_rhs),
        (sep_noise_h, sep_noise),
        (blocks_h, blocks),
        (dev_h, dev),
        (sep_dev_h, sep_dev),
    ]
    for i in (6, 0, 1, 4, 5, 2, 3, 7, 8):
        src, dst = loads[i]
        pltpu.make_async_copy(src, dst, ld_sem.at[i]).start()

    def loaded(i):
        pltpu.make_async_copy(loads[i][0], loads[i][1], ld_sem.at[i]).wait()

    place = lax.broadcasted_iota(jnp.int32, (128, 128), 0) + 32 * (sec & 3)
    lane = lax.broadcasted_iota(jnp.int32, (128, 128), 1)
    turn = jnp.where(lane == (place & 127), F32(1), F32(0)).astype(BF)
    turn_edge = turn[:SEP]
    mine = pl.ds(pl.multiple_of(sec * SAMP, SAMP), SAMP)

    loaded(6)
    dead = ROWS - blocks[0, 0] * BLOCK
    row_id = lax.broadcasted_iota(jnp.int32, (ROWS, 128), 0)
    loaded(0)
    rhs_v[...] = jnp.where(row_id >= dead, rhs_v[...].astype(F32), F32(0)).astype(BF)
    loaded(1)
    live_edge = lax.broadcasted_iota(jnp.int32, (SEP, 128), 0) + edge >= dead
    y_edge = dot(d_v[pl.ds(edge, SEP), :], rhs_v[...], 1, 0)
    y_edge = jnp.where(live_edge, y_edge, F32(0)).astype(BF)
    c1_src[...] = dot(y_edge, turn_edge, 0, 0).astype(BF)
    c1_buf[sec] = c1_src[mine, :]

    loaded(4)
    loaded(5)
    first = jnp.concatenate([sep_rhs[0], sep_noise[0], sep_rhs[1], sep_rhs[2]], axis=0)
    second = jnp.concatenate([sep_noise[1], sep_noise[2]], axis=0)
    rn_src[:, :128] = dot(first, turn, 0, 0).astype(BF)
    rn_src[:, 128:] = dot(second, turn[: 2 * SEP], 0, 0).astype(BF)
    rn_buf[sec] = rn_src[mine, :]

    pl.semaphore_wait(barrier, len(peers))

    def part(ref, sec_mask):
        return ref.at[pl.ds(pl.multiple_of((sec ^ sec_mask) * SAMP, SAMP), SAMP)]

    for leaf_mask in (1, 0):
        for m in SEC_PEERS + ((0,) if leaf_mask else ()):
            send(part(c1_src, m), c1_buf.at[SECS * leaf_mask + sec], c1_s, c1_r, leaf_mask, m)
    for m in SEC_PEERS + (0,):
        send(part(rn_src.at[:, pl.ds(0, 128)], m), rp_buf.at[sec], rp_s, rp_r, 1, m)
    for m in SEC_PEERS:
        send(part(rn_src, m), rn_buf.at[sec], rn_s, rn_r, 0, m)

    chunks = []
    for height, (p, q) in enumerate(((p1, q1), (p2, q2), (p3, q3)), 1):
        cols = pl.ds((2**height - 2) * SPAN, 2**height * SPAN)
        chunks += [(sep_panel.at[:, cols], p), (sep_inv.at[:, cols], q)]

    def rows_of(j, leaf_mask, sec_mask):
        start = (sec ^ sec_mask) * SEP
        if j < 2:
            start += ((leaf ^ leaf_mask) & 1) * SPAN
        return pl.ds(pl.multiple_of(start, SEP), SEP)

    def sources(j):
        return [(0, m) for m in X_PEERS] + ([(1, m) for m in (0,) + X_PEERS] if j < 2 else [])

    for j, (src, dst) in enumerate(chunks):
        own = dst.at[rows_of(j, 0, 0)]
        for i, (leaf_mask, sec_mask) in enumerate(sources(j)):
            send(src, own, mat_s.at[j], x_r.at[j, i], leaf_mask, sec_mask)
        send(src, own, mat_s.at[j], d_r.at[j], 0, 1)
        pltpu.make_async_copy(src, own, own_sem.at[j]).start()

    def forward(j):
        dst = chunks[j][1]
        for i, (leaf_mask, sec_mask) in enumerate(sources(j)):
            block = dst.at[rows_of(j, leaf_mask, sec_mask)]
            wait(block, x_r.at[j, i])
            send(block, block, mat_s.at[j], d_r.at[j], 0, 1)

    def ready(j):
        src, dst = chunks[j]
        pltpu.make_async_copy(src, dst.at[rows_of(j, 0, 0)], own_sem.at[j]).wait()
        wait(dst.at[pl.ds(0, (len(sources(j)) + 1) * SEP)], d_r.at[j])
        return dst

    loaded(2)
    loaded(3)
    loaded(7)
    loaded(8)
    for t in range(4):
        rows = pl.ds(256 * t, 256)
        live = lax.broadcasted_iota(jnp.int32, (256, 128), 0) + 256 * t
        y = dot(d_v[rows, :], rhs_v[...], 1, 0).astype(BF).astype(F32)
        w = y + noise_v[rows, :].astype(F32)
        w_v[rows, :] = jnp.where((live >= dead) & (live < edge), w, F32(0)).astype(BF)
    for t in range(4):
        rows = pl.ds(256 * t, 256)
        x_v[rows, :] = dot(d_v[:, rows], w_v[...], 0, 0)
    eye = lax.broadcasted_iota(jnp.int32, (128, 128), 0) == lane
    for t in range(8):
        rows = pl.ds(128 * t, 128)
        diag = jnp.where(eye, jnp.broadcast_to(dev[t : t + 1, :].astype(F32), (128, 128)), F32(0))
        live = lax.broadcasted_iota(jnp.int32, (128, 128), 0) + 128 * t >= dead
        scale = jnp.broadcast_to(jnp.sum(diag, axis=1, keepdims=True), (128, 128))
        scale_v[rows, :] = jnp.where(live, scale, F32(0))

    wait(rn_buf.at[pl.ds(0, 7)], rn_r)
    wait(rp_buf, rp_r)
    group = lax.broadcasted_iota(jnp.int32, (SAMP, 128), 1) // SEP

    def unpack(item, buf, tile, j):
        for half in range(2):
            got = jnp.zeros((SAMP, 128), F32)
            for s in range(4):
                piece = buf[4 * half + s, :, 128 * tile : 128 * tile + 128].astype(F32)
                got = jnp.where(group == (j + s) % 4, piece, got)
            if j:
                got = pltpu.roll(got, 128 - SEP * j, 1)
            item_v[item, :, 128 * half : 128 * half + 128] = got

    for item, (buf, tile, j) in enumerate(
        ((rn_buf, 0, 0), (rp_buf, 0, 0), (rn_buf, 0, 2), (rn_buf, 0, 3),
         (rn_buf, 0, 1), (rp_buf, 0, 1), (rn_buf, 1, 0), (rn_buf, 1, 1))
    ):
        unpack(item, buf, tile, j)

    forward(0)
    forward(1)
    wait(c1_buf.at[pl.ds(0, 15)], c1_r)

    def cols_of(height, mask):
        return pl.ds(pl.multiple_of(((leaf ^ mask) & (2**height - 1)) * SPAN, SPAN), SPAN)

    def publish(e, height, value):
        f_buf[e, 0] = value
        for m in reversed(NEAR[height]):
            send(f_buf.at[e, 0], f_buf.at[e, m], f_s.at[e], f_r.at[e, m], m, 0)

    def gathered_product(e, height, j):
        matrix = ready(j)
        total = dot(f_buf[e, 0], matrix[:, cols_of(height, 0)], 1, 1)
        for m in NEAR[height]:
            wait(f_buf.at[e, m], f_r.at[e, m])
            total += dot(f_buf[e, m], matrix[:, cols_of(height, m)], 1, 1)
        return total

    def pair_block(matrix, row_mask, col_mask):
        return matrix[cols_of(1, row_mask), cols_of(1, col_mask)]

    children = []
    for leaf_mask in range(2):
        halves = []
        for half in range(2):
            pieces = [c1_buf[SECS * leaf_mask + 4 * half + s].astype(F32) for s in range(4)]
            halves.append((pieces[0] + pieces[1]) + (pieces[2] + pieces[3]))
        children.append(jnp.concatenate(halves, axis=1).astype(BF))
    ready(0)
    reduced = []
    for m in range(2):
        total = dot(children[0], pair_block(p1, m, 0), 1, 1) + dot(children[1], pair_block(p1, m, 1), 1, 1)
        reduced.append((item_v[m] - total).astype(BF))
    ready(1)
    first_solved = []
    for m in range(2):
        total = dot(reduced[0], pair_block(q1, m, 0), 1, 1) + dot(reduced[1], pair_block(q1, m, 1), 1, 1)
        first_solved.append(total.astype(BF))
        f_buf[0, m] = first_solved[m]
    send(f_buf.at[0, pl.ds(0, 2)], f_buf.at[0, pl.ds(2, 2)], f_s.at[0], f_r.at[0, 0], 3, 0)
    forward(2)

    matrix = ready(2)
    total = dot(f_buf[0, 0], matrix[:, cols_of(2, 0)], 1, 1) + dot(f_buf[0, 1], matrix[:, cols_of(2, 1)], 1, 1)
    wait(f_buf.at[0, pl.ds(2, 2)], f_r.at[0, 0])
    total += dot(f_buf[0, 2], matrix[:, cols_of(2, 3)], 1, 1) + dot(f_buf[0, 3], matrix[:, cols_of(2, 2)], 1, 1)
    publish(1, 2, (item_v[2] - total).astype(BF))
    forward(3)
    second_solved = gathered_product(1, 2, 3).astype(BF)
    publish(2, 3, second_solved)
    forward(4)
    total = gathered_product(2, 3, 4)
    publish(3, 3, (item_v[3] - total).astype(BF))
    forward(5)
    third_solved = gathered_product(3, 3, 5).astype(BF)

    def scattered_product(e, height, j, vector):
        matrix = chunks[j][1]
        for m in reversed(NEAR[height]):
            b_src[e, m] = dot(vector, matrix[:, cols_of(height, m)], 1, 0).astype(BF)
            send(b_src.at[e, m], b_buf.at[e, m], b_s.at[e], b_r.at[e, m], m, 0)
        total = dot(vector, matrix[:, cols_of(height, 0)], 1, 0)
        for m in NEAR[height]:
            wait(b_buf.at[e, m], b_r.at[e, m])
            total += b_buf[e, m].astype(F32)
        return total

    def give_back(level, value):
        for half in range(2):
            o_src[level, half] = value[:, 128 * half : 128 * half + 128]
        o_buf[level, sec] = o_src[level, sec >> 2]
        for m in SEC_PEERS:
            send(o_src.at[level, (sec ^ m) >> 2], o_buf.at[level, sec], o_s.at[level], o_r.at[level], 0, m)

    def write_sample(level):
        wait(o_buf.at[level, pl.ds(0, 7)], o_r.at[level])
        flat = o_buf[level].reshape(128, 128)
        mine = dot(turn_edge, flat, 1, 1)
        row = jnp.broadcast_to(sep_dev[level : level + 1, :].astype(F32), (SEP, SEP))
        small = lax.broadcasted_iota(jnp.int32, (SEP, SEP), 0) == lax.broadcasted_iota(jnp.int32, (SEP, SEP), 1)
        scale = jnp.sum(jnp.where(small, row, F32(0)), axis=1, keepdims=True)
        sep_out[level] = (jnp.broadcast_to(scale, (SEP, 128)) * mine).astype(BF)

    vector = (third_solved.astype(F32) + item_v[7]).astype(BF)
    backed = scattered_product(0, 3, 5, vector).astype(BF)
    minus = scattered_product(1, 3, 4, backed)
    give_back(2, backed)
    vector = (second_solved.astype(F32) + item_v[6] - minus).astype(BF)
    backed = scattered_product(2, 2, 3, vector).astype(BF)
    blocks_out = {}
    for m in (2, 3, 1, 0):
        blocks_out[m] = dot(backed, p2[:, cols_of(2, m)], 1, 0)
        b_wide[m] = blocks_out[m].astype(BF)
    for m in (2, 3, 1):
        send(b_wide.at[m], b_near.at[m, 0], w_s, w_r.at[m], m, 0)
        send(b_wide.at[m ^ 1], b_near.at[m, 1], w_s, w_r.at[m], m, 0)
    sums = [blocks_out[0], blocks_out[1]]
    for m in (1, 3, 2):
        wait(b_near.at[m], w_r.at[m])
        for n in range(2):
            sums[n] += b_near[m, n].astype(F32)
    give_back(1, backed)
    vectors = [(first_solved[m].astype(F32) + item_v[4 + m] - sums[m]).astype(BF) for m in range(2)]
    backs = []
    for m in range(2):
        total = dot(vectors[0], pair_block(q1, 0, m), 1, 0) + dot(vectors[1], pair_block(q1, 1, m), 1, 0)
        backs.append(total.astype(BF))
    pushed = dot(backs[0], pair_block(p1, 0, 0), 1, 0) + dot(backs[1], pair_block(p1, 1, 0), 1, 0)
    for half in range(2):
        s_src[half] = pushed[:, 128 * half : 128 * half + 128].astype(BF)
    for m in SEC_PEERS:
        send(s_src.at[(sec ^ m) >> 2], s_buf.at[sec], s_s, s_r, 0, m)
    s_buf[sec] = s_src[sec >> 2]
    backed = backs[0]
    give_back(0, backed)
    write_sample(2)
    write_sample(1)
    wait(s_buf.at[pl.ds(0, 7)], s_r)
    s0 = dot(turn_edge, s_buf[...].reshape(128, 128), 1, 1)
    w_edge = y_edge.astype(F32) + noise_v[pl.ds(edge, SEP), :].astype(F32) - s0
    w_edge = jnp.where(live_edge, w_edge, F32(0)).astype(BF)
    for t in range(4):
        rows = pl.ds(256 * t, 256)
        x = x_v[rows, :] + dot(d_v[pl.ds(edge, SEP), rows], w_edge, 0, 0)
        out[rows, :] = (scale_v[rows, :] * x).astype(BF)
    write_sample(0)

    wait(c1_buf.at[pl.ds(0, 15)], c1_s)
    wait(rn_buf.at[pl.ds(0, 7)], rn_s)
    wait(rp_buf, rp_s)
    for j, (_, dst) in enumerate(chunks):
        wait(dst.at[pl.ds(0, (2 * len(sources(j)) + 1) * SEP)], mat_s.at[j])
    wait(f_buf.at[0, pl.ds(0, 2)], f_s.at[0])
    for e, height in ((1, 2), (2, 3), (3, 3)):
        wait(f_buf.at[e, pl.ds(0, 2**height - 1)], f_s.at[e])
    for e, height in ((0, 3), (1, 3), (2, 2)):
        wait(b_buf.at[e, pl.ds(0, 2**height - 1)], b_s.at[e])
    wait(b_near.at[pl.ds(0, 3)], w_s)
    for level in range(3):
        wait(o_buf.at[level, pl.ds(0, 7)], o_s.at[level])
    wait(s_buf.at[pl.ds(0, 7)], s_s)


def hand_out(leaf_made, sep_made, leaf_out, sep_out, sem):
    pairs = ((leaf_made, leaf_out), (sep_made, sep_out))
    for i, (src, dst) in enumerate(pairs):
        pltpu.make_async_copy(src, dst, sem.at[i]).start()
    for i, (src, dst) in enumerate(pairs):
        pltpu.make_async_copy(src, dst, sem.at[i]).wait()


def on_device(leaf_inv, blocks, rhs, noise, dev, sep_inv, sep_panel, sep_rhs, sep_noise, sep_dev):
    dma = pltpu.SemaphoreType.DMA
    vmem = pltpu.VMEM
    anywhere = pl.BlockSpec(memory_space=pltpu.HBM)
    held = pl.BlockSpec(memory_space=vmem)
    scratch = [
        pltpu.SMEM((1, 1), jnp.int32), vmem((8, 128), BF), vmem((3, SEP, 128), BF), vmem((3, SEP, 128), BF), vmem((3, SEP), BF),
        vmem((ROWS, ROWS), BF), vmem((ROWS, 128), BF), vmem((ROWS, 128), BF), vmem((ROWS, 128), BF),
        vmem((ROWS, 128), F32), vmem((ROWS, 128), F32),
    ]
    for height in (1, 2, 3):
        scratch += [vmem((SPAN * (2 if height == 1 else 1), 2**height * SPAN), BF)] * 2
    scratch += [
        vmem((128, 128), BF), vmem((2 * SECS, SAMP, 128), BF),
        vmem((128, 256), BF), vmem((SECS, SAMP, 256), BF), vmem((SECS, SAMP, 128), BF), vmem((8, SAMP, SPAN), F32),
        vmem((4, 8, SAMP, SPAN), BF), vmem((3, 8, SAMP, SPAN), BF), vmem((3, 8, SAMP, SPAN), BF),
        vmem((4, SAMP, SPAN), BF), vmem((4, 2, SAMP, SPAN), BF),
        vmem((3, 2, SAMP, 128), BF), vmem((3, SECS, SAMP, 128), BF),
        vmem((2, SAMP, 128), BF), vmem((SECS, SAMP, 128), BF),
    ]
    scratch += [
        dma((9,)), dma, dma, dma, dma, dma, dma, dma((6,)), dma((6, 7)), dma((6,)), dma((6,)),
        dma((4,)), dma((4, 8)), dma((3,)), dma((3, 8)), dma, dma((4,)), dma((3,)), dma((3,)), dma, dma,
    ]
    operands = [leaf_inv, rhs, noise, dev.reshape(8, 128), sep_inv, sep_panel, sep_rhs, sep_noise, sep_dev]
    operands = [pltpu.with_memory_space_constraint(a, pltpu.HBM) for a in operands]
    results = (jax.ShapeDtypeStruct(rhs.shape, BF), jax.ShapeDtypeStruct(sep_rhs.shape, BF))
    made = pl.pallas_call(
        kernel,
        out_shape=results,
        in_specs=[anywhere] * 10,
        out_specs=(held, held),
        scratch_shapes=scratch,
        compiler_params=pltpu.CompilerParams(
            collective_id=0, has_side_effects=True, vmem_limit_bytes=30 * 2**20
        ),
    )(operands[0], blocks, *operands[1:])
    return pl.pallas_call(
        hand_out,
        out_shape=results,
        in_specs=[pl.BlockSpec(memory_space=pl.ANY)] * 2,
        out_specs=[pl.BlockSpec(memory_space=pl.ANY)] * 2,
        scratch_shapes=[dma((2,))],
        compiler_params=pltpu.CompilerParams(vmem_limit_bytes=2**20),
    )(*made)


def solution(mesh):
    both = ("leaf", "sec")
    in_specs = (
        P(both, None), P("leaf", "sec"), P(both, None), P(both, None), P(both),
        P(both, None), P(both, None), P(None, both, None), P(None, both, None), P(None, both),
    )
    return jax.shard_map(
        on_device, mesh=mesh, in_specs=in_specs,
        out_specs=(P(both, None), P(None, both, None)), check_vma=False,
    )
```

time: 69.8 us -> 60.5 us (0.87)
  local copies, waits for them, and re-layouts: 9.5 us -> 0 us
    unnamed x20 -> x0, local copies, waits for them, and re-layouts: 9.5 us -> none
    pallas_call x1 -> x2, Pallas kernels: 58.5 us -> 59.1 us  [the longest x1 58.4 us: on_device(): pl.pallas_call(kernel, out_shape=results, in_specs=[anywhere] * 10, out_s...]
where the time goes in v2:
time: 60.5 us; the launch traced here: 60.4 us
  Pallas kernels  59.1 us (98%)
  between operations  1.29 us (2%)
    pallas_call x1, Pallas kernels, on_device(): pl.pallas_call(kernel, out_shape=results, in_specs=[anywhere] * 10, out_s...  58.4 us

profile of v2, /device:TPU:1, one launch (start us, length us, event | category | flops | bytes accessed | tf_op | source)
XLA Modules:
  0.0 60.4 jit_solution(1720827986584287793)
XLA Ops:
  1.3 58.4 %shard_map.113 = (bf16[1024,128]{1,0:T(8,128)(2,1)S(1)}, bf16[3,32,128]{2,1,0:T(8,128)(2,1)S(1)}) custom-call(bf16[1024,1024]{1,0:T(8,128)(2,1)} %leaf_inv.1, s32[1,1]{1,0:T(1,128)S(6)} %copy.12.blocks_h, bf16[1024,128]{1,0:T(8,128)(2,1)} %rhs.1, bf16[1024,128]{1,0:T(8,128)(2,1)} %noise.1, bf16[8,128]{1,0:T(8,128)(2,1)} %bitcast.1, ...), custom_call_target="tpu_custom_call" | custom-call | tf_op jit(solution)/shard_map/pallas_call | solution.py:370
  59.6 0.7 %shard_map.114 = (bf16[1024,128]{1,0:T(8,128)(2,1)}, bf16[3,32,128]{2,1,0:T(8,128)(2,1)}) custom-call(bf16[1024,128]{1,0:T(8,128)(2,1)S(1)} %get-tuple-element.4.leaf_made, bf16[3,32,128]{2,1,0:T(8,128)(2,1)S(1)} %get-tuple-element.5.sep_made), custom_call_target="tpu_custom_call" | custom-call | tf_op jit(solution)/shard_map/pallas_call | solution.py:380

commit v3 on v2

v3 whole, which is shorter than its diff:
```python
import functools

import jax
import jax.numpy as jnp
from jax import lax
from jax.experimental import pallas as pl
from jax.experimental.pallas import tpu as pltpu
from jax.sharding import PartitionSpec as P

MESH = pl.DeviceIdType.MESH
BLOCK = 128
BF = jnp.bfloat16
F32 = jnp.float32
ROWS = 1024
SEP = 32
SECS = 8
SPAN = SECS * SEP
SAMP = 16
NEAR = {1: (1,), 2: (1, 3, 2), 3: (1, 3, 4, 2, 5, 7, 6)}
SEC_PEERS = (6, 4, 7, 5, 2, 3, 1)
PAIR = ((1, 0), (0, 2), (0, 6), (0, 4), (1, 2), (1, 6), (1, 4))
GREET = ((1, 4), (1, 2), (1, 6), (0, 4), (1, 0), (0, 2), (0, 6), (3, 0), (4, 0), (0, 1))


def dot(a, b, ca, cb):
    return lax.dot_general(a, b, (((ca,), (cb,)), ((), ())), preferred_element_type=F32)


def kernel(
    leaf_inv, blocks_h, rhs, noise, dev_h, sep_inv, sep_panel, sep_rhs_h, sep_noise_h, sep_dev_h,
    out, sep_out,
    blocks, dev, sep_rhs, sep_noise, sep_dev, d_v, rhs_v, noise_v, w_v, x_v, scale_v,
    p1, q1, p2, q2, p3, q3,
    e_src, e_got, e_mix, own_buf, pair_buf, item_v, f_buf, b_src, b_buf, b_wide, b_near, o_src, o_buf, s_src, s_buf,
    ld_sem, swap_s, swap_r, line_s, line_r, pair_s, pair_r, own_sem, x_r, d_r, mat_s, f_s, f_r, b_s, b_r, w_s, w_r,
    o_s, o_r, s_s, s_r,
):
    leaf = lax.axis_index("leaf")
    sec = lax.axis_index("sec")

    def at(leaf_mask, sec_mask):
        return (leaf ^ leaf_mask, sec ^ sec_mask)

    def send(src, dst, send_sem, recv_sem, leaf_mask, sec_mask):
        pltpu.make_async_remote_copy(
            src_ref=src, dst_ref=dst, send_sem=send_sem, recv_sem=recv_sem,
            device_id=at(leaf_mask, sec_mask), device_id_type=MESH,
        ).start()

    def wait(ref, sem):
        pltpu.make_async_copy(ref, ref, sem).wait()

    barrier = pltpu.get_barrier_semaphore()
    for leaf_mask, sec_mask in GREET:
        pl.semaphore_signal(barrier, inc=1, device_id=at(leaf_mask, sec_mask), device_id_type=MESH)

    edge = ROWS - SEP
    loads = [
        (rhs, rhs_v),
        (leaf_inv.at[pl.ds(edge, SEP)], d_v.at[pl.ds(edge, SEP)]),
        (leaf_inv.at[pl.ds(0, edge)], d_v.at[pl.ds(0, edge)]),
        (noise, noise_v),
        (sep_rhs_h, sep_rhs),
        (sep_noise_h, sep_noise),
        (blocks_h, blocks),
        (dev_h, dev),
        (sep_dev_h, sep_dev),
    ]
    for i in (6, 0, 1, 4, 5, 2, 3, 7, 8):
        src, dst = loads[i]
        pltpu.make_async_copy(src, dst, ld_sem.at[i]).start()

    def loaded(i):
        pltpu.make_async_copy(loads[i][0], loads[i][1], ld_sem.at[i]).wait()

    core, chip = sec & 1, sec >> 1
    k = lax.broadcasted_iota(jnp.int32, (2 * SEP, 128), 0)
    place = (k & 31) + SEP * core + 64 * (((k >> 5) + chip) & 1)
    lane = lax.broadcasted_iota(jnp.int32, (2 * SEP, 128), 1)
    turn = jnp.where(lane == place, F32(1), F32(0)).astype(BF)
    turn_edge = turn[:SEP]

    loaded(6)
    dead = ROWS - blocks[0, 0] * BLOCK
    row_id = lax.broadcasted_iota(jnp.int32, (ROWS, 128), 0)
    loaded(0)
    rhs_v[...] = jnp.where(row_id >= dead, rhs_v[...].astype(F32), F32(0)).astype(BF)
    loaded(1)
    live_edge = lax.broadcasted_iota(jnp.int32, (SEP, 128), 0) + edge >= dead
    y_edge = dot(d_v[pl.ds(edge, SEP), :], rhs_v[...], 1, 0)
    y_edge = jnp.where(live_edge, y_edge, F32(0)).astype(BF)
    loaded(4)
    loaded(5)
    e_src[:, :, :, :128] = dot(y_edge, turn_edge, 0, 0).astype(BF).reshape(4, 2, SAMP, 128)
    for tile, rows in enumerate(((sep_rhs[0], sep_noise[0]), (sep_rhs[1], sep_rhs[2]), (sep_noise[1], sep_noise[2])), 1):
        turned = dot(jnp.concatenate(rows, axis=0), turn, 0, 0).astype(BF)
        e_src[:, :, :, 128 * tile : 128 * tile + 128] = turned.reshape(4, 2, SAMP, 128)

    pl.semaphore_wait(barrier, len(GREET))
    send(e_src.at[:, 1 - core], e_got, swap_s, swap_r, 0, 1)

    chunks = []
    for height, (p, q) in enumerate(((p1, q1), (p2, q2), (p3, q3)), 1):
        cols = pl.ds((2**height - 2) * SPAN, 2**height * SPAN)
        chunks += [(sep_panel.at[:, cols], p), (sep_inv.at[:, cols], q)]

    chunks.append(chunks[1])

    def sources(j):
        return PAIR if j == 0 else (PAIR[:1] + PAIR[4:] if j == 6 else PAIR[1:4])

    def rows_of(j, leaf_mask, sec_mask):
        start = (sec ^ sec_mask) * SEP
        if j in (0, 1, 6):
            start += ((leaf ^ leaf_mask) & 1) * SPAN
        return pl.ds(pl.multiple_of(start, SEP), SEP)

    def spread(j):
        src, dst = chunks[j]
        own = dst.at[rows_of(j, 0, 0)]
        for i, (leaf_mask, sec_mask) in enumerate(sources(j)):
            send(src, own, mat_s.at[j], x_r.at[j, i], leaf_mask, sec_mask)
        if j < 6:
            send(src, own, mat_s.at[j], d_r.at[j], 0, 1)
            pltpu.make_async_copy(src, own, own_sem.at[j]).start()

    def forward(j):
        for i, (leaf_mask, sec_mask) in enumerate(sources(j)):
            block = chunks[j][1].at[rows_of(j, leaf_mask, sec_mask)]
            wait(block, x_r.at[j, i])
            send(block, block, mat_s.at[j], d_r.at[j], 0, 1)

    def ready(j):
        src, dst = chunks[j]
        if j < 6:
            pltpu.make_async_copy(src, dst.at[rows_of(j, 0, 0)], own_sem.at[j]).wait()
        wait(dst.at[pl.ds(0, (len(sources(j)) + (j < 6)) * SEP)], d_r.at[j])
        return dst

    spread(0)
    spread(1)

    def give_edge(leaf_mask, sec_mask):
        src = e_mix.at[chip ^ (sec_mask >> 1)]
        if leaf_mask:
            send(src.at[:, pl.ds(0, 256)], pair_buf.at[chip], pair_s, pair_r, leaf_mask, sec_mask)
        else:
            send(src, own_buf.at[chip], line_s, line_r, leaf_mask, sec_mask)

    wait(e_got, swap_r)
    e_mix[...] = (e_src[:, core].astype(F32) + e_got[...].astype(F32)).astype(BF)
    own_buf[chip] = e_mix[chip]
    for leaf_mask, sec_mask in reversed(PAIR):
        give_edge(leaf_mask, sec_mask)
    for j in range(2, 7):
        spread(j)
    forward(0)
    forward(1)

    def leaf_solve():
        loaded(2)
        loaded(3)
        for t in range(4):
            rows = pl.ds(256 * t, 256)
            live = lax.broadcasted_iota(jnp.int32, (256, 128), 0) + 256 * t
            y = dot(d_v[rows, :], rhs_v[...], 1, 0).astype(BF).astype(F32)
            w = y + noise_v[rows, :].astype(F32)
            w_v[rows, :] = jnp.where((live >= dead) & (live < edge), w, F32(0)).astype(BF)

    def leaf_back():
        for t in range(4):
            rows = pl.ds(256 * t, 256)
            x_v[rows, :] = dot(d_v[:, rows], w_v[...], 0, 0)

    def leaf_scale():
        loaded(7)
        loaded(8)
        row = lax.broadcasted_iota(jnp.int32, (128, 128), 0)
        eye = row == lax.broadcasted_iota(jnp.int32, (128, 128), 1)
        for t in range(8):
            diag = jnp.where(eye, jnp.broadcast_to(dev[t : t + 1, :].astype(F32), (128, 128)), F32(0))
            scale = jnp.broadcast_to(jnp.sum(diag, axis=1, keepdims=True), (128, 128))
            scale_v[pl.ds(128 * t, 128), :] = jnp.where(row + 128 * t >= dead, scale, F32(0))

    wait(own_buf.at[pl.ds(0, 3)], line_r)
    wait(pair_buf, pair_r)
    group = lax.broadcasted_iota(jnp.int32, (SAMP, 128), 1) // 64

    def unpack(item, buf, tile, f):
        cols = slice(128 * tile, 128 * tile + 128)
        for half in range(2):
            got = jnp.where(group == f, buf[2 * half, :, cols].astype(F32), buf[2 * half + 1, :, cols].astype(F32))
            if f:
                got = pltpu.roll(got, 64, 1)
            item_v[item, :, 128 * half : 128 * half + 128] = got

    children = []
    for buf in (own_buf, pair_buf):
        tiles = [buf[c, :, :128].astype(F32) for c in range(4)]
        children.append(jnp.concatenate([tiles[0] + tiles[1], tiles[2] + tiles[3]], axis=1).astype(BF))
    for item, (buf, tile, f) in enumerate(
        ((own_buf, 1, 0), (pair_buf, 1, 0), (own_buf, 2, 0), (own_buf, 2, 1),
         (own_buf, 1, 1), (pair_buf, 1, 1), (own_buf, 3, 0), (own_buf, 3, 1))
    ):
        unpack(item, buf, tile, f)

    def cols_of(height, mask):
        return pl.ds(pl.multiple_of(((leaf ^ mask) & (2**height - 1)) * SPAN, SPAN), SPAN)

    def publish(e, height, value):
        f_buf[e, 0] = value
        for m in reversed(NEAR[height]):
            send(f_buf.at[e, 0], f_buf.at[e, m], f_s.at[e], f_r.at[e, m], m, 0)

    def gathered_product(e, height, j):
        matrix = ready(j)
        total = dot(f_buf[e, 0], matrix[:, cols_of(height, 0)], 1, 1)
        for part in (NEAR[height][:3], NEAR[height][3:]):
            for m in part:
                wait(f_buf.at[e, m], f_r.at[e, m])
            for m in part:
                total += dot(f_buf[e, m], matrix[:, cols_of(height, m)], 1, 1)
        return total

    def pair_block(matrix, row_mask, col_mask):
        return matrix[cols_of(1, row_mask), cols_of(1, col_mask)]

    ready(0)
    reduced = []
    for m in range(2):
        total = dot(children[0], pair_block(p1, m, 0), 1, 1) + dot(children[1], pair_block(p1, m, 1), 1, 1)
        reduced.append((item_v[m] - total).astype(BF))
    ready(1)
    total = dot(reduced[0], pair_block(q1, 0, 0), 1, 1) + dot(reduced[1], pair_block(q1, 0, 1), 1, 1)
    first_solved = total.astype(BF)
    publish(0, 2, first_solved)
    forward(2)

    total = gathered_product(0, 2, 2)
    publish(1, 2, (item_v[2] - total).astype(BF))
    forward(3)

    leaf_solve()
    second_solved = gathered_product(1, 2, 3).astype(BF)
    publish(2, 3, second_solved)
    forward(4)

    leaf_back()
    total = gathered_product(2, 3, 4)
    publish(3, 3, (item_v[3] - total).astype(BF))
    forward(5)

    forward(6)
    leaf_scale()
    third_solved = gathered_product(3, 3, 5).astype(BF)

    def scattered_product(e, height, j, vector):
        matrix = chunks[j][1]
        for part in (NEAR[height][3:], NEAR[height][:3]):
            for m in reversed(part):
                b_src[e, m] = dot(vector, matrix[:, cols_of(height, m)], 1, 0).astype(BF)
            for m in reversed(part):
                send(b_src.at[e, m], b_buf.at[e, m], b_s.at[e], b_r.at[e, m], m, 0)
        total = dot(vector, matrix[:, cols_of(height, 0)], 1, 0)
        for m in NEAR[height]:
            wait(b_buf.at[e, m], b_r.at[e, m])
            total += b_buf[e, m].astype(F32)
        return total

    def give_back(level, value):
        i = level - 1
        for half in range(2):
            o_src[i, half] = value[:, 128 * half : 128 * half + 128]
        o_buf[i, sec] = o_src[i, sec >> 2]
        for m in SEC_PEERS:
            send(o_src.at[i, (sec ^ m) >> 2], o_buf.at[i, sec], o_s.at[i], o_r.at[i], 0, m)

    def put_sample(level, flat):
        mine = dot(turn_edge, flat, 1, 1)
        row = jnp.broadcast_to(sep_dev[level : level + 1, :].astype(F32), (SEP, SEP))
        small = lax.broadcasted_iota(jnp.int32, (SEP, SEP), 0) == lax.broadcasted_iota(jnp.int32, (SEP, SEP), 1)
        scale = jnp.sum(jnp.where(small, row, F32(0)), axis=1, keepdims=True)
        sep_out[level] = (jnp.broadcast_to(scale, (SEP, 128)) * mine).astype(BF)

    def write_sample(level):
        wait(o_buf.at[level - 1, pl.ds(0, 7)], o_r.at[level - 1])
        put_sample(level, o_buf[level - 1].reshape(128, 128))

    vector = (third_solved.astype(F32) + item_v[7]).astype(BF)
    backed = scattered_product(0, 3, 5, vector).astype(BF)
    minus = scattered_product(1, 3, 4, backed)
    give_back(2, backed)
    vector = (second_solved.astype(F32) + item_v[6] - minus).astype(BF)
    backed = scattered_product(2, 2, 3, vector).astype(BF)
    blocks_out = {}
    for m in (2, 3, 1, 0):
        blocks_out[m] = dot(backed, p2[:, cols_of(2, m)], 1, 0)
        b_wide[m] = blocks_out[m].astype(BF)
    for m in (2, 3, 1):
        send(b_wide.at[m], b_near.at[m, 0], w_s, w_r.at[m], m, 0)
        send(b_wide.at[m ^ 1], b_near.at[m, 1], w_s, w_r.at[m], m, 0)
    sums = [blocks_out[0], blocks_out[1]]
    for m in (1, 3, 2):
        wait(b_near.at[m], w_r.at[m])
        for n in range(2):
            sums[n] += b_near[m, n].astype(F32)
    give_back(1, backed)
    ready(6)
    vectors = [(f_buf[0, m].astype(F32) + item_v[4 + m] - sums[m]).astype(BF) for m in range(2)]
    backs = []
    for m in range(2):
        total = dot(vectors[0], pair_block(q1, 0, m), 1, 0) + dot(vectors[1], pair_block(q1, 1, m), 1, 0)
        backs.append(total.astype(BF))
    pushed = dot(backs[0], pair_block(p1, 0, 0), 1, 0) + dot(backs[1], pair_block(p1, 1, 0), 1, 0)
    for half in range(2):
        s_src[half, 0] = pushed[:, 128 * half : 128 * half + 128].astype(BF)
        s_src[half, 1] = backs[0][:, 128 * half : 128 * half + 128]
    for m in SEC_PEERS:
        send(s_src.at[(sec ^ m) >> 2], s_buf.at[sec], s_s, s_r, 0, m)
    s_buf[sec] = s_src[sec >> 2]
    write_sample(2)
    write_sample(1)
    wait(e_got, swap_s)
    wait(own_buf.at[pl.ds(0, 3)], line_s)
    wait(pair_buf, pair_s)
    for j, (_, dst) in enumerate(chunks):
        wait(dst.at[pl.ds(0, (2 * len(sources(j)) + (j < 6)) * SEP)], mat_s.at[j])
    for e, height in ((0, 2), (1, 2), (2, 3), (3, 3)):
        wait(f_buf.at[e, pl.ds(0, 2**height - 1)], f_s.at[e])
    for e, height in ((0, 3), (1, 3), (2, 2)):
        wait(b_buf.at[e, pl.ds(0, 2**height - 1)], b_s.at[e])
    wait(b_near.at[pl.ds(0, 3)], w_s)
    for level in (1, 2):
        wait(o_buf.at[level - 1, pl.ds(0, 7)], o_s.at[level - 1])
    wait(s_buf.at[pl.ds(0, 7)], s_r)
    s0 = dot(turn_edge, s_buf[:, 0].reshape(128, 128), 1, 1)
    w_edge = y_edge.astype(F32) + noise_v[pl.ds(edge, SEP), :].astype(F32) - s0
    w_edge = jnp.where(live_edge, w_edge, F32(0)).astype(BF)
    for t in range(4):
        rows = pl.ds(256 * t, 256)
        x = x_v[rows, :] + dot(d_v[pl.ds(edge, SEP), rows], w_edge, 0, 0)
        out[rows, :] = (scale_v[rows, :] * x).astype(BF)
    put_sample(0, s_buf[:, 1].reshape(128, 128))
    wait(s_buf.at[pl.ds(0, 7)], s_s)


def hand_out(leaf_made, sep_made, leaf_out, sep_out, sem):
    pairs = ((leaf_made, leaf_out), (sep_made, sep_out))
    for i, (src, dst) in enumerate(pairs):
        pltpu.make_async_copy(src, dst, sem.at[i]).start()
    for i, (src, dst) in enumerate(pairs):
        pltpu.make_async_copy(src, dst, sem.at[i]).wait()


def on_device(leaf_inv, blocks, rhs, noise, dev, sep_inv, sep_panel, sep_rhs, sep_noise, sep_dev):
    dma = pltpu.SemaphoreType.DMA
    vmem = pltpu.VMEM
    anywhere = pl.BlockSpec(memory_space=pltpu.HBM)
    held = pl.BlockSpec(memory_space=vmem)
    scratch = [
        pltpu.SMEM((1, 1), jnp.int32), vmem((8, 128), BF), vmem((3, SEP, 128), BF), vmem((3, SEP, 128), BF), vmem((3, SEP), BF),
        vmem((ROWS, ROWS), BF), vmem((ROWS, 128), BF), vmem((ROWS, 128), BF), vmem((ROWS, 128), BF),
        vmem((ROWS, 128), F32), vmem((ROWS, 128), F32),
    ]
    for height in (1, 2, 3):
        scratch += [vmem((SPAN * (2 if height == 1 else 1), 2**height * SPAN), BF)] * 2
    scratch += [
        vmem((4, 2, SAMP, 512), BF), vmem((4, SAMP, 512), BF), vmem((4, SAMP, 512), BF), vmem((4, SAMP, 512), BF),
        vmem((4, SAMP, 256), BF), vmem((8, SAMP, SPAN), F32),
        vmem((4, 8, SAMP, SPAN), BF), vmem((3, 8, SAMP, SPAN), BF), vmem((3, 8, SAMP, SPAN), BF),
        vmem((4, SAMP, SPAN), BF), vmem((4, 2, SAMP, SPAN), BF),
        vmem((2, 2, SAMP, 128), BF), vmem((2, SECS, SAMP, 128), BF),
        vmem((2, 2, SAMP, 128), BF), vmem((SECS, 2, SAMP, 128), BF),
    ]
    scratch += [
        dma((9,)), dma, dma, dma, dma, dma, dma, dma((6,)), dma((7, 7)), dma((7,)), dma((7,)),
        dma((4,)), dma((4, 8)), dma((3,)), dma((3, 8)), dma, dma((4,)), dma((2,)), dma((2,)), dma, dma,
    ]
    operands = [leaf_inv, rhs, noise, dev.reshape(8, 128), sep_inv, sep_panel, sep_rhs, sep_noise, sep_dev]
    operands = [pltpu.with_memory_space_constraint(a, pltpu.HBM) for a in operands]
    results = (jax.ShapeDtypeStruct(rhs.shape, BF), jax.ShapeDtypeStruct(sep_rhs.shape, BF))
    made = pl.pallas_call(
        kernel,
        out_shape=results,
        in_specs=[anywhere] * 10,
        out_specs=(held, held),
        scratch_shapes=scratch,
        compiler_params=pltpu.CompilerParams(
            collective_id=0, has_side_effects=True, vmem_limit_bytes=30 * 2**20
        ),
    )(operands[0], blocks, *operands[1:])
    return pl.pallas_call(
        hand_out,
        out_shape=results,
        in_specs=[pl.BlockSpec(memory_space=pl.ANY)] * 2,
        out_specs=[pl.BlockSpec(memory_space=pl.ANY)] * 2,
        scratch_shapes=[dma((2,))],
        compiler_params=pltpu.CompilerParams(vmem_limit_bytes=2**20),
    )(*made)


def solution(mesh):
    both = ("leaf", "sec")
    in_specs = (
        P(both, None), P("leaf", "sec"), P(both, None), P(both, None), P(both),
        P(both, None), P(both, None), P(None, both, None), P(None, both, None), P(None, both),
    )
    return jax.shard_map(
        on_device, mesh=mesh, in_specs=in_specs,
        out_specs=(P(both, None), P(None, both, None)), check_vma=False,
    )
```

time: 60.5 us -> 58.9 us (0.974)
  Pallas kernels: 59.1 us -> 57.4 us
    pallas_call x1, Pallas kernels: 58.4 us -> 56.7 us  [on_device(): pl.pallas_call(kernel, out_shape=results, in_specs=[anywhere] * 10, out_s...]
where the time goes in v3:
time: 58.9 us; the launch traced here: 58.7 us
  Pallas kernels  57.4 us (97%)
  between operations  1.29 us (2%)
    pallas_call x1, Pallas kernels, on_device(): pl.pallas_call(kernel, out_shape=results, in_specs=[anywhere] * 10, out_s...  56.7 us

profile of v3, /device:TPU:1, one launch (start us, length us, event | category | flops | bytes accessed | tf_op | source)
XLA Modules:
  0.0 58.7 jit_solution(6536457687711961098)
XLA Ops:
  1.3 56.7 %shard_map.113 = (bf16[1024,128]{1,0:T(8,128)(2,1)S(1)}, bf16[3,32,128]{2,1,0:T(8,128)(2,1)S(1)}) custom-call(bf16[1024,1024]{1,0:T(8,128)(2,1)} %leaf_inv.1, s32[1,1]{1,0:T(1,128)S(6)} %copy.12.blocks_h, bf16[1024,128]{1,0:T(8,128)(2,1)} %rhs.1, bf16[1024,128]{1,0:T(8,128)(2,1)} %noise.1, bf16[8,128]{1,0:T(8,128)(2,1)} %bitcast.1, ...), custom_call_target="tpu_custom_call" | custom-call | tf_op jit(solution)/shard_map/pallas_call | solution.py:382
  58.0 0.7 %shard_map.114 = (bf16[1024,128]{1,0:T(8,128)(2,1)}, bf16[3,32,128]{2,1,0:T(8,128)(2,1)}) custom-call(bf16[1024,128]{1,0:T(8,128)(2,1)S(1)} %get-tuple-element.4.leaf_made, bf16[3,32,128]{2,1,0:T(8,128)(2,1)S(1)} %get-tuple-element.5.sep_made), custom_call_target="tpu_custom_call" | custom-call | tf_op jit(solution)/shard_map/pallas_call | solution.py:392

commit v4 on v3

--- a/solution.py
+++ b/solution.py
@@ -198,11 +198,8 @@
     for buf in (own_buf, pair_buf):
         tiles = [buf[c, :, :128].astype(F32) for c in range(4)]
         children.append(jnp.concatenate([tiles[0] + tiles[1], tiles[2] + tiles[3]], axis=1).astype(BF))
-    for item, (buf, tile, f) in enumerate(
-        ((own_buf, 1, 0), (pair_buf, 1, 0), (own_buf, 2, 0), (own_buf, 2, 1),
-         (own_buf, 1, 1), (pair_buf, 1, 1), (own_buf, 3, 0), (own_buf, 3, 1))
-    ):
-        unpack(item, buf, tile, f)
+    unpack(0, own_buf, 1, 0)
+    unpack(1, pair_buf, 1, 0)
 
     def cols_of(height, mask):
         return pl.ds(pl.multiple_of(((leaf ^ mask) & (2**height - 1)) * SPAN, SPAN), SPAN)
@@ -234,11 +231,17 @@
     total = dot(reduced[0], pair_block(q1, 0, 0), 1, 1) + dot(reduced[1], pair_block(q1, 0, 1), 1, 1)
     first_solved = total.astype(BF)
     publish(0, 2, first_solved)
+    unpack(2, own_buf, 2, 0)
+    unpack(3, own_buf, 2, 1)
     forward(2)
 
     total = gathered_product(0, 2, 2)
     publish(1, 2, (item_v[2] - total).astype(BF))
     forward(3)
+    unpack(4, own_buf, 1, 1)
+    unpack(5, pair_buf, 1, 1)
+    unpack(6, own_buf, 3, 0)
+    unpack(7, own_buf, 3, 1)
 
     leaf_solve()
     second_solved = gathered_product(1, 2, 3).astype(BF)
@@ -254,7 +257,7 @@
     leaf_scale()
     third_solved = gathered_product(3, 3, 5).astype(BF)
 
-    def scattered_product(e, height, j, vector):
+    def scattered_product(e, height, j, vector, meanwhile=None):
         matrix = chunks[j][1]
         for part in (NEAR[height][3:], NEAR[height][:3]):
             for m in reversed(part):
@@ -262,6 +265,8 @@
             for m in reversed(part):
                 send(b_src.at[e, m], b_buf.at[e, m], b_s.at[e], b_r.at[e, m], m, 0)
         total = dot(vector, matrix[:, cols_of(height, 0)], 1, 0)
+        if meanwhile is not None:
+            meanwhile()
         for m in NEAR[height]:
             wait(b_buf.at[e, m], b_r.at[e, m])
             total += b_buf[e, m].astype(F32)
@@ -289,9 +294,9 @@
     vector = (third_solved.astype(F32) + item_v[7]).astype(BF)
     backed = scattered_product(0, 3, 5, vector).astype(BF)
     minus = scattered_product(1, 3, 4, backed)
-    give_back(2, backed)
     vector = (second_solved.astype(F32) + item_v[6] - minus).astype(BF)
-    backed = scattered_product(2, 2, 3, vector).astype(BF)
+    top_backed = backed
+    backed = scattered_product(2, 2, 3, vector, lambda: give_back(2, top_backed)).astype(BF)
     blocks_out = {}
     for m in (2, 3, 1, 0):
         blocks_out[m] = dot(backed, p2[:, cols_of(2, m)], 1, 0)
@@ -299,12 +304,12 @@
     for m in (2, 3, 1):
         send(b_wide.at[m], b_near.at[m, 0], w_s, w_r.at[m], m, 0)
         send(b_wide.at[m ^ 1], b_near.at[m, 1], w_s, w_r.at[m], m, 0)
+    give_back(1, backed)
     sums = [blocks_out[0], blocks_out[1]]
     for m in (1, 3, 2):
         wait(b_near.at[m], w_r.at[m])
         for n in range(2):
             sums[n] += b_near[m, n].astype(F32)
-    give_back(1, backed)
     ready(6)
     vectors = [(f_buf[0, m].astype(F32) + item_v[4 + m] - sums[m]).astype(BF) for m in range(2)]
     backs = []

time: 58.9 us -> 58.8 us (level)
  no operation moved by 1% of the time
where the time goes in v4:
time: 58.8 us; the launch traced here: 58.7 us
  Pallas kernels  57.4 us (98%)
  between operations  1.29 us (2%)
    pallas_call x1, Pallas kernels, on_device(): pl.pallas_call(kernel, out_shape=results, in_specs=[anywhere] * 10, out_s...  56.7 us

profile of v4, /device:TPU:1, one launch (start us, length us, event | category | flops | bytes accessed | tf_op | source)
XLA Modules:
  0.0 58.7 jit_solution(2514153665214236958)
XLA Ops:
  1.3 56.7 %shard_map.113 = (bf16[1024,128]{1,0:T(8,128)(2,1)S(1)}, bf16[3,32,128]{2,1,0:T(8,128)(2,1)S(1)}) custom-call(bf16[1024,1024]{1,0:T(8,128)(2,1)} %leaf_inv.1, s32[1,1]{1,0:T(1,128)S(6)} %copy.12.blocks_h, bf16[1024,128]{1,0:T(8,128)(2,1)} %rhs.1, bf16[1024,128]{1,0:T(8,128)(2,1)} %noise.1, bf16[8,128]{1,0:T(8,128)(2,1)} %bitcast.1, ...), custom_call_target="tpu_custom_call" | custom-call | tf_op jit(solution)/shard_map/pallas_call | solution.py:387
  58.0 0.7 %shard_map.114 = (bf16[1024,128]{1,0:T(8,128)(2,1)}, bf16[3,32,128]{2,1,0:T(8,128)(2,1)}) custom-call(bf16[1024,128]{1,0:T(8,128)(2,1)S(1)} %get-tuple-element.4.leaf_made, bf16[3,32,128]{2,1,0:T(8,128)(2,1)S(1)} %get-tuple-element.5.sep_made), custom_call_target="tpu_custom_call" | custom-call | tf_op jit(solution)/shard_map/pallas_call | solution.py:397

commit v5 on v4

--- a/solution.py
+++ b/solution.py
@@ -154,8 +154,6 @@
         give_edge(leaf_mask, sec_mask)
     for j in range(2, 7):
         spread(j)
-    forward(0)
-    forward(1)
 
     def leaf_solve():
         loaded(2)
@@ -200,6 +198,8 @@
         children.append(jnp.concatenate([tiles[0] + tiles[1], tiles[2] + tiles[3]], axis=1).astype(BF))
     unpack(0, own_buf, 1, 0)
     unpack(1, pair_buf, 1, 0)
+    forward(0)
+    forward(1)
 
     def cols_of(height, mask):
         return pl.ds(pl.multiple_of(((leaf ^ mask) & (2**height - 1)) * SPAN, SPAN), SPAN)

time: 58.8 us -> 58.8 us (level)
  no operation moved by 1% of the time
where the time goes in v5:
time: 58.8 us; the launch traced here: 58.7 us
  Pallas kernels  57.4 us (98%)
  between operations  1.29 us (2%)
    pallas_call x1, Pallas kernels, on_device(): pl.pallas_call(kernel, out_shape=results, in_specs=[anywhere] * 10, out_s...  56.7 us

profile of v5, /device:TPU:1, one launch (start us, length us, event | category | flops | bytes accessed | tf_op | source)
XLA Modules:
  0.0 58.7 jit_solution(15114550737958311015)
XLA Ops:
  1.3 56.7 %shard_map.113 = (bf16[1024,128]{1,0:T(8,128)(2,1)S(1)}, bf16[3,32,128]{2,1,0:T(8,128)(2,1)S(1)}) custom-call(bf16[1024,1024]{1,0:T(8,128)(2,1)} %leaf_inv.1, s32[1,1]{1,0:T(1,128)S(6)} %copy.12.blocks_h, bf16[1024,128]{1,0:T(8,128)(2,1)} %rhs.1, bf16[1024,128]{1,0:T(8,128)(2,1)} %noise.1, bf16[8,128]{1,0:T(8,128)(2,1)} %bitcast.1, ...), custom_call_target="tpu_custom_call" | custom-call | tf_op jit(solution)/shard_map/pallas_call | solution.py:387
  58.0 0.7 %shard_map.114 = (bf16[1024,128]{1,0:T(8,128)(2,1)}, bf16[3,32,128]{2,1,0:T(8,128)(2,1)}) custom-call(bf16[1024,128]{1,0:T(8,128)(2,1)S(1)} %get-tuple-element.4.leaf_made, bf16[3,32,128]{2,1,0:T(8,128)(2,1)S(1)} %get-tuple-element.5.sep_made), custom_call_target="tpu_custom_call" | custom-call | tf_op jit(solution)/shard_map/pallas_call | solution.py:397
